TPU v7x, 512 devices: a whole 4x4x16 slice. The times are simulated.
512 devices in a mesh: sky: 16 (over y, x), sensor: 32 (over z, core).
Axes of the slice: x: 4, y: 4, z: 16, core: 2. Of those that a mesh axis runs over, the one named last changes fastest.
Arguments:
- sky: bfloat16 [146, 512], P(None, 'sky'), may hold values from 0.049804688 to 5
- daylight: bfloat16 [32, 640, 145, 146], P('sensor', 'sky'), may hold values from -0.5 to 0.5
- bsdf: bfloat16 [32, 145, 145], P('sensor'), may hold values from -0.5 to 0.5
- bsdf_ids: int32 [32, 640], P('sensor', 'sky'), may hold values from 0 to 31
- view: bfloat16 [32, 256, 32, 145], P('sensor', 'sky'), may hold values from -0.125 to 0.125
- visible: int32 [32, 256, 32], P('sensor', 'sky'), may hold values from 0 to 639, as said below
- counts: int32 [32, 256], P('sensor', 'sky'), may hold values from 1 to 32, 4096 in all within a row
Outputs:
- illuminance: float32 [32, 512, 256], P('sensor', 'sky')
Inputs may be any that keep to these rules, and one draw needn't show every extreme that they name: `visible`: each sensor lists 32 different windows of its own tile. `counts`: the lists of one tile hold 4096 live entries in all.
All inputs are finite; a program needn't handle non-finite values. No bound on the sum of `counts` on one device may be relied on, other than what follows from the above.
Results may differ from a plain program's by a relative error of at most 0.004.
Values may be sent and summed in bfloat16 or wider, within the bound.
A program may use at most 128 MiB of HBM per device.

v0:
```python
import math

import jax
import jax.numpy as jnp
from jax import lax
from jax.sharding import PartitionSpec as P


def body(sky, daylight, bsdf, bsdf_ids, view, visible, counts):
    local_day = daylight[0]
    sky_devices = lax.axis_size("sky")
    irradiance = jnp.einsum(
        "wbp,ph->whb",
        local_day,
        lax.all_gather(sky, "sky", axis=1, tiled=True),
        preferred_element_type=jnp.float32,
    ).astype(jnp.bfloat16)
    tables = lax.all_gather(bsdf, "sensor", axis=0, tiled=True)
    chosen = tables[bsdf_ids[0]]
    transmitted = jnp.einsum(
        "whb,wcb->whc", irradiance, chosen, preferred_element_type=jnp.float32
    ).astype(jnp.bfloat16)
    slot_count = view.shape[2]
    slot_index = lax.broadcasted_iota(jnp.int32, visible.shape, 2)
    live = slot_index < counts[:, :, None]
    live_view = jnp.where(live[:, :, :, None], view, jnp.zeros_like(view))
    rows_all, ids_all = (
        lax.all_gather(live_view, "sky", axis=1, tiled=True),
        lax.all_gather(visible, "sky", axis=1, tiled=True),
    )
    rows_all = rows_all[0]
    ids_all = ids_all[0]
    sens_tile = rows_all.shape[0]
    hours = transmitted.shape[1]
    hour_dev = hours // sky_devices
    light = lax.all_to_all(transmitted, "sky", split_axis=1, concat_axis=0, tiled=True)
    block = math.gcd(sens_tile, 32)
    blocks = sens_tile // block
    rows_blocked = rows_all.reshape(blocks, block, slot_count, rows_all.shape[2])
    ids_blocked = ids_all.reshape(blocks, block, slot_count)

    def sensor_block(items):
        coeffs, window_ids = items
        picked = light[window_ids]
        return jnp.einsum("skhb,skb->hs", picked, coeffs, preferred_element_type=jnp.float32)

    parts_out = lax.map(sensor_block, (rows_blocked, ids_blocked))
    illuminance = jnp.transpose(parts_out, (1, 0, 2)).reshape(hour_dev, sens_tile)
    return illuminance[None]


def solution(mesh):
    in_specs = (
        P(None, "sky"),
        P("sensor", "sky", None, None),
        P("sensor", None, None),
        P("sensor", "sky"),
        P("sensor", "sky", None, None),
        P("sensor", "sky", None),
        P("sensor", "sky"),
    )
    out_specs = P("sensor", "sky", None)
    return jax.shard_map(body, mesh=mesh, in_specs=in_specs, out_specs=out_specs, check_vma=False)
```

profile of v0, /device:TPU:1, one launch (start us, length us, event | category | flops | bytes accessed | tf_op | source)
XLA Modules:
  0.0 534.1 jit_solution(2210962505744205326)
XLA Ops:
  8.1 19.8 %all_gather.14 = bf16[146,512]{0,1:T(8,128)(2,1)S(1)} all-gather(bf16[146,32]{0,1:T(8,128)(2,1)} %param.9), channel_id=1, replica_groups=mesh['sky'=16,'sensor'=32] {'sky'}, dimensions={1}, use_global_device_ids=true | all-gather | bytes 158848 | tf_op jit(solution)/shard_map/all_gather | solution.py:15
  28.6 60.0 %all-gather.5.cloned.1.call-done = bf16[32,145,145]{2,1,0:T(8,128)(2,1)} async-done(((bf16[1,145,145]{2,1,0:T(8,128)(2,1)}), bf16[32,145,145]{2,1,0:T(8,128)(2,1)}) %all-gather.5.cloned.1.call-update) | async-done | bytes 1345616 | tf_op jit(solution)/shard_map/all_gather | solution.py:18
  92.9 7.5 %fusion.7 = bf16[40,512,145]{1,2,0:T(8,128)(2,1)} fusion(bf16[40,145,145]{2,1,0:T(8,128)(2,1)} %gather_fusion.1, bf16[40,145,146]{2,0,1:T(8,128)(2,1)S(1)} %bitcast.50, bf16[146,512]{0,1:T(8,128)(2,1)S(1)} %all_gather.14), kind=kOutput, calls=%fused_computation.12 | convolution fusion | flops 1734246400 | bytes 9464304 | tf_op jit(solution)/shard_map/whb,wcb->whc/dot_general | solution.py:20
  100.4 15.9 %copy.18 = bf16[40,512,145]{2,0,1:T(8,128)(2,1)} copy(bf16[40,512,145]{1,2,0:T(8,128)(2,1)} %fusion.7) | data formatting | bytes 11878400 | tf_op jit(solution)/shard_map/convert_element_type | solution.py:22
  116.3 6.5 %all-to-all-start = ((bf16[40,512,145]{2,0,1:T(8,128)(2,1)}), bf16[40,512,145]{2,0,1:T(8,128)(2,1)}, u32[]{:S(2)}, u32[]{:S(2)}) async-start(bf16[40,512,145]{2,0,1:T(8,128)(2,1)} %copy.18), calls=%async_computation | async-start | bytes 20971520 | tf_op jit(solution)/shard_map/all_to_all | solution.py:36
  123.9 184.5 %all_gather.13 = s32[1,256,32]{2,1,0:T(8,128)S(1)} all-gather(s32[1,16,32]{2,1,0:T(8,128)S(1)} %copy-done.3), channel_id=1, replica_groups=mesh['sky'=16,'sensor'=32] {'sky'}, dimensions={1}, use_global_device_ids=true | all-gather | bytes 34816 | tf_op jit(solution)/shard_map/all_gather | solution.py:29
  308.4 11.0 %copy.20 = bf16[16,40,32,145]{3,2,1,0:T(8,128)(2,1)} copy(bf16[16,40,32,145]{3,1,2,0:T(8,128)(2,1)} %bitcast.18) | data formatting | bytes 11878400 | tf_op jit(solution)/shard_map/all_to_all | solution.py:36
  319.4 205.3 %while.10 = (s32[]{:T(128)}, f32[8,32,32]{2,1,0:T(8,128)S(1)}, bf16[8,32,32,145]{3,2,1,0:T(8,128)(2,1)}, s32[8,32,32]{2,1,0:T(8,128)S(1)}, bf16[640,32,145]{2,1,0:T(8,128)(2,1)}, /*index=5*/s32[]{:T(128)}) while((s32[]{:T(128)}, f32[8,32,32]{2,1,0:T(8,128)S(1)}, bf16[8,32,32,145]{3,2,1,0:T(8,128)(2,1)}, s32[8,32,32]{2,1,0:T(8,128)S(1)}, ...), condition=%wide.region_1.2_spmd, body=%wide.region_0.1_spmd.sunk | while | flops 9506818 | bytes 29472848 | solution.py:47
  319.5 16.3 %gather_fusion = bf16[1024,32,145]{2,1,0:T(8,128)(2,1)} fusion(bf16[640,32,145]{2,1,0:T(8,128)(2,1)} %get-tuple-element.90, s32[1024]{0:T(1024)S(1)} %broadcast_clamp_fusion.2), kind=kCustom, calls=%fused_computation.clone.1 | custom fusion | bytes 19009536 | tf_op jit(solution)/shard_map/while/body/eval_jaxpr/gather | solution.py:44
  337.0 8.0 %fusion.22 = f32[32,1,32,1]{2,1,3,0:T(1,128)S(1)} fusion(bf16[32,32,32,145]{3,2,1,0:T(8,128)(2,1)} %bitcast.52, bf16[32,32,145,1]{2,1,0,3:T(8,128)(2,1)S(1)} %dynamic-slice_bitcast_fusion.2), kind=kOutput, calls=%fused_computation.2.clone.1 | convolution fusion | flops 9502720 | bytes 9803776 | tf_op jit(solution)/shard_map/while/body/eval_jaxpr/skhb,skb->hs/dot_general | solution.py:45
  345.2 16.4 %gather_fusion = bf16[1024,32,145]{2,1,0:T(8,128)(2,1)} fusion(bf16[640,32,145]{2,1,0:T(8,128)(2,1)} %get-tuple-element.90, s32[1024]{0:T(1024)S(1)} %broadcast_clamp_fusion.2), kind=kCustom, calls=%fused_computation.clone.1 | custom fusion | bytes 19009536 | tf_op jit(solution)/shard_map/while/body/eval_jaxpr/gather | solution.py:44
  362.6 8.0 %fusion.22 = f32[32,1,32,1]{2,1,3,0:T(1,128)S(1)} fusion(bf16[32,32,32,145]{3,2,1,0:T(8,128)(2,1)} %bitcast.52, bf16[32,32,145,1]{2,1,0,3:T(8,128)(2,1)S(1)} %dynamic-slice_bitcast_fusion.2), kind=kOutput, calls=%fused_computation.2.clone.1 | convolution fusion | flops 9502720 | bytes 9803776 | tf_op jit(solution)/shard_map/while/body/eval_jaxpr/skhb,skb->hs/dot_general | solution.py:45
  370.9 16.4 %gather_fusion = bf16[1024,32,145]{2,1,0:T(8,128)(2,1)} fusion(bf16[640,32,145]{2,1,0:T(8,128)(2,1)} %get-tuple-element.90, s32[1024]{0:T(1024)S(1)} %broadcast_clamp_fusion.2), kind=kCustom, calls=%fused_computation.clone.1 | custom fusion | bytes 19009536 | tf_op jit(solution)/shard_map/while/body/eval_jaxpr/gather | solution.py:44
  388.3 8.0 %fusion.22 = f32[32,1,32,1]{2,1,3,0:T(1,128)S(1)} fusion(bf16[32,32,32,145]{3,2,1,0:T(8,128)(2,1)} %bitcast.52, bf16[32,32,145,1]{2,1,0,3:T(8,128)(2,1)S(1)} %dynamic-slice_bitcast_fusion.2), kind=kOutput, calls=%fused_computation.2.clone.1 | convolution fusion | flops 9502720 | bytes 9803776 | tf_op jit(solution)/shard_map/while/body/eval_jaxpr/skhb,skb->hs/dot_general | solution.py:45
  396.5 16.4 %gather_fusion = bf16[1024,32,145]{2,1,0:T(8,128)(2,1)} fusion(bf16[640,32,145]{2,1,0:T(8,128)(2,1)} %get-tuple-element.90, s32[1024]{0:T(1024)S(1)} %broadcast_clamp_fusion.2), kind=kCustom, calls=%fused_computation.clone.1 | custom fusion | bytes 19009536 | tf_op jit(solution)/shard_map/while/body/eval_jaxpr/gather | solution.py:44
  414.0 8.0 %fusion.22 = f32[32,1,32,1]{2,1,3,0:T(1,128)S(1)} fusion(bf16[32,32,32,145]{3,2,1,0:T(8,128)(2,1)} %bitcast.52, bf16[32,32,145,1]{2,1,0,3:T(8,128)(2,1)S(1)} %dynamic-slice_bitcast_fusion.2), kind=kOutput, calls=%fused_computation.2.clone.1 | convolution fusion | flops 9502720 | bytes 9803776 | tf_op jit(solution)/shard_map/while/body/eval_jaxpr/skhb,skb->hs/dot_general | solution.py:45
  422.2 16.4 %gather_fusion = bf16[1024,32,145]{2,1,0:T(8,128)(2,1)} fusion(bf16[640,32,145]{2,1,0:T(8,128)(2,1)} %get-tuple-element.90, s32[1024]{0:T(1024)S(1)} %broadcast_clamp_fusion.2), kind=kCustom, calls=%fused_computation.clone.1 | custom fusion | bytes 19009536 | tf_op jit(solution)/shard_map/while/body/eval_jaxpr/gather | solution.py:44
  439.6 8.0 %fusion.22 = f32[32,1,32,1]{2,1,3,0:T(1,128)S(1)} fusion(bf16[32,32,32,145]{3,2,1,0:T(8,128)(2,1)} %bitcast.52, bf16[32,32,145,1]{2,1,0,3:T(8,128)(2,1)S(1)} %dynamic-slice_bitcast_fusion.2), kind=kOutput, calls=%fused_computation.2.clone.1 | convolution fusion | flops 9502720 | bytes 9803776 | tf_op jit(solution)/shard_map/while/body/eval_jaxpr/skhb,skb->hs/dot_general | solution.py:45
  447.8 16.4 %gather_fusion = bf16[1024,32,145]{2,1,0:T(8,128)(2,1)} fusion(bf16[640,32,145]{2,1,0:T(8,128)(2,1)} %get-tuple-element.90, s32[1024]{0:T(1024)S(1)} %broadcast_clamp_fusion.2), kind=kCustom, calls=%fused_computation.clone.1 | custom fusion | bytes 19009536 | tf_op jit(solution)/shard_map/while/body/eval_jaxpr/gather | solution.py:44
  465.3 8.0 %fusion.22 = f32[32,1,32,1]{2,1,3,0:T(1,128)S(1)} fusion(bf16[32,32,32,145]{3,2,1,0:T(8,128)(2,1)} %bitcast.52, bf16[32,32,145,1]{2,1,0,3:T(8,128)(2,1)S(1)} %dynamic-slice_bitcast_fusion.2), kind=kOutput, calls=%fused_computation.2.clone.1 | convolution fusion | flops 9502720 | bytes 9803776 | tf_op jit(solution)/shard_map/while/body/eval_jaxpr/skhb,skb->hs/dot_general | solution.py:45
  473.5 16.4 %gather_fusion = bf16[1024,32,145]{2,1,0:T(8,128)(2,1)} fusion(bf16[640,32,145]{2,1,0:T(8,128)(2,1)} %get-tuple-element.90, s32[1024]{0:T(1024)S(1)} %broadcast_clamp_fusion.2), kind=kCustom, calls=%fused_computation.clone.1 | custom fusion | bytes 19009536 | tf_op jit(solution)/shard_map/while/body/eval_jaxpr/gather | solution.py:44
  490.9 8.0 %fusion.22 = f32[32,1,32,1]{2,1,3,0:T(1,128)S(1)} fusion(bf16[32,32,32,145]{3,2,1,0:T(8,128)(2,1)} %bitcast.52, bf16[32,32,145,1]{2,1,0,3:T(8,128)(2,1)S(1)} %dynamic-slice_bitcast_fusion.2), kind=kOutput, calls=%fused_computation.2.clone.1 | convolution fusion | flops 9502720 | bytes 9803776 | tf_op jit(solution)/shard_map/while/body/eval_jaxpr/skhb,skb->hs/dot_general | solution.py:45
  499.2 16.4 %gather_fusion = bf16[1024,32,145]{2,1,0:T(8,128)(2,1)} fusion(bf16[640,32,145]{2,1,0:T(8,128)(2,1)} %get-tuple-element.90, s32[1024]{0:T(1024)S(1)} %broadcast_clamp_fusion.2), kind=kCustom, calls=%fused_computation.clone.1 | custom fusion | bytes 19009536 | tf_op jit(solution)/shard_map/while/body/eval_jaxpr/gather | solution.py:44
  516.6 8.0 %fusion.22 = f32[32,1,32,1]{2,1,3,0:T(1,128)S(1)} fusion(bf16[32,32,32,145]{3,2,1,0:T(8,128)(2,1)} %bitcast.52, bf16[32,32,145,1]{2,1,0,3:T(8,128)(2,1)S(1)} %dynamic-slice_bitcast_fusion.2), kind=kOutput, calls=%fused_computation.2.clone.1 | convolution fusion | flops 9502720 | bytes 9803776 | tf_op jit(solution)/shard_map/while/body/eval_jaxpr/skhb,skb->hs/dot_general | solution.py:45
  (72 shorter events, 18.5 us)
Async XLA Ops:
  7.4 85.5 %copy-start = (bf16[1,40,145,146]{3,1,2,0:T(8,128)(2,1)S(1)}, bf16[1,40,145,146]{3,1,2,0:T(8,128)(2,1)}, u32[]{:S(2)}) copy-start(bf16[1,40,145,146]{3,1,2,0:T(8,128)(2,1)} %param.10) | copy-start | bytes 5080804
  7.4 81.2 %all-gather.5.cloned.1.call-start = ((), (), s32[]{:S(2)}) async-start(), calls=%async_computation.2 | async-start | bytes 2568192 | tf_op jit(solution)/shard_map/all_gather | solution.py:18
  116.3 6.6 %copy-start.4 = (s32[1,16]{1,0:T(1,128)S(1)}, s32[1,16]{1,0:T(1,128)}, u32[]{:S(2)}) copy-start(s32[1,16]{1,0:T(1,128)} %param.15) | copy-start | bytes 196
  116.3 6.7 %copy-start.2 = (bf16[1,16,32,145]{3,2,1,0:T(8,128)(2,1)S(1)}, bf16[1,16,32,145]{3,2,1,0:T(8,128)(2,1)}, u32[]{:S(2)}) copy-start(bf16[1,16,32,145]{3,2,1,0:T(8,128)(2,1)} %param.13) | copy-start | bytes 445444
  116.3 7.6 %copy-start.3 = (s32[1,16,32]{2,1,0:T(8,128)S(1)}, s32[1,16,32]{2,1,0:T(8,128)}, u32[]{:S(2)}) copy-start(s32[1,16,32]{2,1,0:T(8,128)} %param.14) | copy-start | bytes 6148
  116.3 192.1 %all-to-all-start = ((bf16[40,512,145]{2,0,1:T(8,128)(2,1)}), bf16[40,512,145]{2,0,1:T(8,128)(2,1)}, u32[]{:S(2)}, u32[]{:S(2)}) async-start(bf16[40,512,145]{2,0,1:T(8,128)(2,1)} %copy.18), calls=%async_computation | async-start | bytes 20971520 | tf_op jit(solution)/shard_map/all_to_all | solution.py:36
  122.8 196.6 %all-gather.3.cloned.1.call-start = ((), (), s32[]{:S(2)}) async-start(), calls=%async_computation.1 | async-start | bytes 4456448 | tf_op jit(solution)/shard_map/all_gather | solution.py:28
  524.7 1.9 copy-start.1
Sparse Core Ops, SparseCore 0:
  10.3 78.2 all-gather.4
Sparse Core Ops, SparseCore 1:
  126.3 170.5 all-gather.2
where the time goes:
time: 540 us; the launch traced here: 534 us
  blocking collectives  204 us (38%)
  local copies, waits for them, and re-layouts  174 us (32%)
  matrix products  71.9 us (13%)
  waiting for transfers between devices  60.7 us (11%)
  between operations  14.9 us (3%)
  starting transfers between devices  6.59 us (1%)
    all_gather x1, blocking collectives, body(): lax.all_gather(visible, 'sky', axis=1, tiled=True)  185 us
    gather x8, local copies, waits for them, and re-layouts, sensor_block(): picked = light[window_ids]  131 us
    dot_general x8, matrix products, sensor_block(): jnp.einsum('skhb,skb->hs', picked, coeffs, preferred_element_type=jnp.flo...  64.4 us
    all_gather x1, waiting for transfers between devices, body(): tables = lax.all_gather(bsdf, 'sensor', axis=0, tiled=True)  60 us
    all_gather x1, blocking collectives, body(): lax.all_gather(sky, 'sky', axis=1, tiled=True)  19.8 us
    convert_element_type x1, local copies, waits for them, and re-layouts, body(): transmitted = jnp.einsum('whb,wcb->whc', irradiance, chosen, preferred_el...  15.9 us
    all_to_all x1, local copies, waits for them, and re-layouts, body(): lax.all_to_all(transmitted, 'sky', split_axis=1, concat_axis=0, tiled=True)  11 us
  transfers between devices with their start and end apart: 3, of which 1 were waited for; matrix products, arithmetic and copies ran while one was open for 2% of the time, Pallas kernels for 0%

commit v1 on v0

v1 whole, which is shorter than its diff:
```python
import math

import jax
import jax.numpy as jnp
from jax import lax
from jax.experimental import pallas as pl
from jax.experimental.pallas import tpu as pltpu
from jax.sharding import PartitionSpec as P

F32 = jnp.float32
BF16 = jnp.bfloat16
MESH = pl.DeviceIdType.MESH
ROWS = 48
META = 16


def up(n, m):
    return -(-n // m) * m


def iota(shape, dim):
    return lax.broadcasted_iota(jnp.int32, shape, dim)


def dot(a, b, dims=((1,), (0,))):
    return lax.dot_general(a, b, (dims, ((), ())), preferred_element_type=F32)


def kernel(dims, sky_ref, day_hbm, bsdf_ref, ids_ref, view_ref, vis_ref, counts_ref, out_ref, flag_ref,
           day, wide, days, mats, tables, own, vpad, rank, send, got, dense, part, chunks, total, whole,
           day_sem, loc_sem, ring_send, ring_recv, sib_send, sib_recv, v_send, v_recv, a_send, a_recv, g_send, g_recv):
    n_sky, n_sen, bins, patches, wins, sens, slots = dims
    nz = n_sen // 2
    kb = up(bins, 16)
    entries = sens * slots
    me = lax.axis_index("sky")
    mine = lax.axis_index("sensor")
    z, core = mine // 2, lax.rem(mine, 2)
    after = lax.rem(z + 1, nz) * 2 + core
    before = lax.rem(z + nz - 1, nz) * 2 + core
    sibling = z * 2 + (1 - core)

    barrier = pltpu.get_barrier_semaphore()

    def greet(k, c):
        pl.semaphore_signal(barrier, inc=1, device_id=(lax.rem(me + k, n_sky), mine), device_id_type=MESH)
        return c

    lax.fori_loop(1, n_sky, greet, 0)
    for other in (after, before, sibling):
        pl.semaphore_signal(barrier, inc=1, device_id=(me, other), device_id_type=MESH)

    day_copy = pltpu.make_async_copy(day_hbm, day, day_sem)
    day_copy.start()

    vis = vis_ref[...]
    owner = vis // wins
    local = vis - owner * wins
    spread = (lax.rem(iota((slots, entries), 1), slots) == iota((slots, entries), 0)).astype(BF16)
    sensor_of = iota((sens, entries), 1) // slots == iota((sens, entries), 0)

    def flat(x):
        return jnp.sum(jnp.where(sensor_of, dot(x.astype(F32).astype(BF16), spread), 0.0), axis=0, keepdims=True)

    owner_row, local_row = flat(owner), flat(local)
    slot_row = lax.rem(iota((1, entries), 1), slots).astype(F32)
    sens_row = (iota((1, entries), 1) // slots).astype(F32)
    counts = jnp.broadcast_to(counts_ref[...].astype(F32), (16, sens)).astype(BF16)
    count_row = dot(counts, sensor_of.astype(BF16))[0:1]
    live = slot_row < count_row
    goes = jnp.logical_and(iota((n_sky, entries), 0).astype(F32) == owner_row, live)
    goes_f = goes.astype(F32)
    earlier = (iota((entries, entries), 0) < iota((entries, entries), 1)).astype(BF16)
    rank[...] = jnp.where(goes, dot(goes_f.astype(BF16), earlier), -1.0)
    most = jnp.max(jnp.sum(goes_f, axis=1, keepdims=True), axis=0, keepdims=True)
    over = jnp.where(most > ROWS, 1.0, 0.0)

    own[...] = jnp.zeros(own.shape, BF16)
    own[0:bins, 0:bins] = bsdf_ref[...]
    corner = own[kb - 16 : kb, 128:256].astype(F32)
    last = jnp.logical_and(iota(corner.shape, 0) == 15, iota(corner.shape, 1) == 127)
    own[kb - 16 : kb, 128:256] = jnp.where(last, over, corner).astype(BF16)

    pl.semaphore_wait(barrier, n_sky + 2)

    def table(src, at, device, s_sem, r_sem):
        return pltpu.make_async_remote_copy(
            src_ref=src, dst_ref=tables.at[at], send_sem=s_sem, recv_sem=r_sem, device_id=(me, device), device_id_type=MESH)

    own_copy = pltpu.make_async_copy(own, tables.at[mine], loc_sem.at[0])
    own_copy.start()
    sent = []

    def go(copy):
        copy.start()
        sent.append(copy)

    def at_z(shift):
        return lax.rem(z + shift + nz, nz) * 2 + core

    right_steps, left_steps = nz // 2, nz - 1 - nz // 2

    def ring(step):
        for steps, sign, to, lane in ((right_steps, -1, after, 0), (left_steps, 1, before, 1)):
            if step > steps:
                continue
            at = at_z(sign * step)
            src = own if step == 0 else tables.at[at]
            if step > 0:
                table(src, at, mine_other(sign), ring_send.at[lane, 0], ring_recv.at[at // 2]).wait_recv()
            if step < steps:
                go(table(src, at, to, ring_send.at[lane, step], ring_recv.at[at // 2]))
            if step > 0 or lane == 0:
                go(table(src, at, sibling, sib_send.at[at // 2], sib_recv.at[at // 2]))

    def mine_other(sign):
        return before if sign < 0 else after

    steps_done = [0]

    def ring_next():
        if steps_done[0] <= right_steps:
            ring(steps_done[0])
        steps_done[0] += 1

    ring_next()

    vpad[...] = jnp.zeros(vpad.shape, BF16)
    vpad[:, 0:bins] = view_ref[...]
    meta_row = iota((META, entries), 0)
    meta = jnp.where(meta_row == 0, local_row + 1.0, jnp.where(meta_row == 1, sens_row, 0.0)).astype(BF16)
    place = iota((ROWS, entries), 0).astype(F32)

    def pack(q, c):
        pick = (place == rank[pl.ds(q, 1), :]).astype(BF16)
        send[q, 0:ROWS, :] = dot(pick, vpad[...]).astype(BF16)
        send[q, ROWS : ROWS + META, 0:ROWS] = dot(meta, pick, ((1,), (1,))).astype(BF16)
        return c

    lax.fori_loop(0, n_sky, pack, 0)

    def message(q, slot):
        return pltpu.make_async_remote_copy(
            src_ref=send.at[q], dst_ref=got.at[slot], send_sem=v_send.at[q], recv_sem=v_recv.at[slot],
            device_id=(q, mine), device_id_type=MESH)

    def put(k, c):
        message(lax.rem(me + k, n_sky), me).start()
        return c

    lax.fori_loop(1, n_sky, put, 0)
    keep = pltpu.make_async_copy(send.at[me], got.at[me], loc_sem.at[1])
    keep.start()
    ring_next()

    wide[1] = jnp.zeros(wide.shape[1:], F32)
    wide[0, bins * wins :, :] = jnp.zeros((wide.shape[1] - bins * wins, 128), F32)
    day_copy.wait()

    def widen(b, c):
        x = day[b].astype(F32)
        rows = pl.ds(pl.multiple_of(b * wins, 8), wins)
        wide[0, rows, :] = x[:, 0:128]
        wide[1, rows, 0 : patches - 128] = x[:, 128:patches]
        return c

    lax.fori_loop(0, bins, widen, 0, unroll=5 if bins % 5 == 0 else 1)
    ring_next()

    def by_window(w, c):
        for half in range(2):
            days[w, :, half * 128 : half * 128 + 128] = wide[half, pl.ds(w, kb, stride=wins), :].astype(BF16)
        return c

    lax.fori_loop(0, wins, by_window, 0)
    ring_next()

    keep.wait()

    def await_message(k, c):
        message(lax.rem(me + k, n_sky), lax.rem(me + k, n_sky)).wait_recv()
        return c

    lax.fori_loop(1, n_sky, await_message, 0)
    ring_next()
    which = iota((wins * sens, ROWS), 0).astype(F32)

    def unpack(q, c):
        note = got[q, ROWS : ROWS + META, 0:ROWS].astype(F32)
        code = note[0:1] * float(sens) + note[1:2] - float(sens)
        pick = (which == code).astype(BF16)
        rows = dot(pick, got[q, 0:ROWS, :]).astype(BF16).reshape(wins, sens, 256)
        dense[:, pl.ds(pl.multiple_of(q * sens, sens), sens), :] = rows
        return c

    lax.fori_loop(0, n_sky // 2, unpack, 0)
    ring_next()
    lax.fori_loop(n_sky // 2, n_sky, unpack, 0)
    while steps_done[0] <= right_steps:
        ring_next()
    own_copy.wait()

    def await_sibling(i, c):
        at = i * 2 + (1 - core)
        table(tables.at[at], at, sibling, sib_send.at[i], sib_recv.at[i]).wait_recv()
        return c

    lax.fori_loop(0, nz, await_sibling, 0)

    def through(w, c):
        mats[w] = dot(tables[ids_ref[0, w]][:, 0:kb], days[w]).astype(BF16)
        return c

    lax.fori_loop(0, wins, through, 0, unroll=4)

    part[...] = jnp.zeros(part.shape, F32)
    group = 8 if wins % 8 == 0 else 1

    def gather(g, c):
        acc = part[...]
        for i in range(group):
            w = g * group + i
            acc = acc + dot(dense[w][:, 0:kb], mats[w])
        part[...] = acc
        return c

    lax.fori_loop(0, wins // group, gather, 0)
    flags = jnp.zeros((16, 128), F32)
    for i in range(n_sen):
        flags = flags + tables[i, kb - 16 : kb, 128:256].astype(F32)
    any_over = jnp.where(flags[15:16, 127:128] > 0.0, 1.0, 0.0)
    lane = iota((sens * n_sky, 256), 1)
    part[...] = jnp.where(lane < patches, part[...], jnp.where(lane == 255, any_over, 0.0))

    def share(q, slot):
        return pltpu.make_async_remote_copy(
            src_ref=part.at[pl.ds(pl.multiple_of(q * sens, sens), sens)], dst_ref=chunks.at[slot],
            send_sem=a_send.at[q], recv_sem=a_recv.at[slot], device_id=(q, mine), device_id_type=MESH)

    def put_share(k, c):
        share(lax.rem(me + k, n_sky), me).start()
        return c

    lax.fori_loop(1, n_sky, put_share, 0)
    total[...] = part[pl.ds(pl.multiple_of(me * sens, sens), sens), :]

    def add(k, c):
        q = lax.rem(me + k, n_sky)
        share(q, q).wait_recv()
        total[...] += chunks[q]
        return c

    lax.fori_loop(1, n_sky, add, 0)

    def spread_out(q, slot):
        return pltpu.make_async_remote_copy(
            src_ref=total, dst_ref=whole.at[pl.ds(pl.multiple_of(slot * sens, sens), sens)],
            send_sem=g_send.at[q], recv_sem=g_recv.at[slot], device_id=(q, mine), device_id_type=MESH)

    def put_total(k, c):
        spread_out(lax.rem(me + k, n_sky), me).start()
        return c

    lax.fori_loop(1, n_sky, put_total, 0)
    whole[pl.ds(pl.multiple_of(me * sens, sens), sens), :] = total[...]

    def await_total(k, c):
        q = lax.rem(me + k, n_sky)
        spread_out(q, q).wait_recv()
        return c

    lax.fori_loop(1, n_sky, await_total, 0)
    a = whole[...]
    high = a.astype(BF16)
    low = (a - high.astype(F32)).astype(BF16)
    sky = sky_ref[...]
    out_ref[...] = dot(sky, high[:, 0:patches], ((1,), (1,))) + dot(sky, low[:, 0:patches], ((1,), (1,)))
    flag_ref[...] = jnp.broadcast_to(total[0:1, 255:256], flag_ref.shape)

    for copy in sent:
        copy.wait_send()

    def drain(k, c):
        q = lax.rem(me + k, n_sky)
        message(q, me).wait_send()
        share(q, me).wait_send()
        spread_out(q, me).wait_send()
        return c

    lax.fori_loop(1, n_sky, drain, 0)


def general(sky, daylight, bsdf, bsdf_ids, view, visible, counts):
    local_day = daylight[0]
    sky_devices = lax.axis_size("sky")
    irradiance = jnp.einsum(
        "wbp,ph->whb", local_day, lax.all_gather(sky, "sky", axis=1, tiled=True), preferred_element_type=F32
    ).astype(BF16)
    tables = lax.all_gather(bsdf, "sensor", axis=0, tiled=True)
    chosen = tables[bsdf_ids[0]]
    transmitted = jnp.einsum("whb,wcb->whc", irradiance, chosen, preferred_element_type=F32).astype(BF16)
    slot_count = view.shape[2]
    slot_index = lax.broadcasted_iota(jnp.int32, visible.shape, 2)
    live = slot_index < counts[:, :, None]
    live_view = jnp.where(live[:, :, :, None], view, jnp.zeros_like(view))
    rows_all = lax.all_gather(live_view, "sky", axis=1, tiled=True)[0]
    ids_all = lax.all_gather(visible, "sky", axis=1, tiled=True)[0]
    sens_tile = rows_all.shape[0]
    hour_dev = transmitted.shape[1] // sky_devices
    light = lax.all_to_all(transmitted, "sky", split_axis=1, concat_axis=0, tiled=True)
    block = math.gcd(sens_tile, 32)
    blocks = sens_tile // block
    rows_blocked = rows_all.reshape(blocks, block, slot_count, rows_all.shape[2])
    ids_blocked = ids_all.reshape(blocks, block, slot_count)

    def sensor_block(items):
        coeffs, window_ids = items
        return jnp.einsum("skhb,skb->hs", light[window_ids], coeffs, preferred_element_type=F32)

    parts_out = lax.map(sensor_block, (rows_blocked, ids_blocked))
    return jnp.transpose(parts_out, (1, 0, 2)).reshape(hour_dev, sens_tile)


def body(sky, daylight, bsdf, bsdf_ids, view, visible, counts):
    n_sky, n_sen = lax.axis_size("sky"), lax.axis_size("sensor")
    patches, hours = sky.shape
    _, wins, bins, _ = daylight.shape
    _, sens, slots, _ = view.shape
    kb, entries, nz = up(bins, 16), sens * slots, n_sen // 2
    dims = (n_sky, n_sen, bins, patches, wins, sens, slots)
    vmem = pl.BlockSpec(memory_space=pltpu.VMEM)
    dma = pltpu.SemaphoreType.DMA

    def run(*refs):
        kernel(dims, *refs)

    out, flag = pl.pallas_call(
        run,
        out_shape=(jax.ShapeDtypeStruct((hours, sens * n_sky), F32), jax.ShapeDtypeStruct((8, 128), F32)),
        in_specs=[vmem, pl.BlockSpec(memory_space=pl.ANY), vmem, pl.BlockSpec(memory_space=pltpu.SMEM), vmem, vmem, vmem],
        out_specs=(vmem, vmem),
        scratch_shapes=[
            pltpu.VMEM((bins, wins, patches), BF16),
            pltpu.VMEM((2, kb * wins, 128), F32),
            pltpu.VMEM((wins, kb, 256), BF16),
            pltpu.VMEM((wins, kb, 256), BF16),
            pltpu.VMEM((n_sen, kb, 256), BF16),
            pltpu.VMEM((kb, 256), BF16),
            pltpu.VMEM((entries, 256), BF16),
            pltpu.VMEM((n_sky, entries), F32),
            pltpu.VMEM((n_sky, ROWS + META, 256), BF16),
            pltpu.VMEM((n_sky, ROWS + META, 256), BF16),
            pltpu.VMEM((wins, sens * n_sky, 256), BF16),
            pltpu.VMEM((sens * n_sky, 256), F32),
            pltpu.VMEM((n_sky, sens, 256), F32),
            pltpu.VMEM((sens, 256), F32),
            pltpu.VMEM((sens * n_sky, 256), F32),
            dma, dma((2,)), dma((2, nz)), dma((nz,)), dma((nz,)), dma((nz,)),
            dma((n_sky,)), dma((n_sky,)), dma((n_sky,)), dma((n_sky,)), dma((n_sky,)), dma((n_sky,)),
        ],
        compiler_params=pltpu.CompilerParams(collective_id=0, has_side_effects=True, vmem_limit_bytes=56 * 2**20),
    )(
        sky.T,
        jnp.transpose(daylight[0], (1, 0, 2)),
        bsdf[0],
        bsdf_ids,
        view[0].reshape(entries, bins),
        visible[0],
        counts,
    )
    result = lax.cond(
        flag[0, 0] > 0.0,
        lambda: general(sky, daylight, bsdf, bsdf_ids, view, visible, counts),
        lambda: out,
    )
    return result[None]


def solution(mesh):
    in_specs = (
        P(None, "sky"),
        P("sensor", "sky", None, None),
        P("sensor", None, None),
        P("sensor", "sky"),
        P("sensor", "sky", None, None),
        P("sensor", "sky", None),
        P("sensor", "sky"),
    )
    return jax.shard_map(body, mesh=mesh, in_specs=in_specs, out_specs=P("sensor", "sky", None), check_vma=False)
```

time: 540 us -> 83.5 us (0.15); the launches traced: 534 us -> 83.4 us
  blocking collectives: 204 us -> 0 us
  local copies, waits for them, and re-layouts: 174 us -> 1.81 us
  matrix products: 71.9 us -> 0 us
  Pallas kernels: 0 us -> 67.3 us
  waiting for transfers between devices: 60.7 us -> 0 us
  starting transfers between devices: 6.59 us -> 0 us
    all_gather x2 -> x0, blocking collectives: 204 us -> none  [the longest x1 185 us: body(): lax.all_gather(visible, 'sky', axis=1, tiled=True)]
    gather x9 -> x0, local copies, waits for them, and re-layouts: 135 us -> none  [the longest x8 131 us: sensor_block(): picked = light[window_ids]]
    dot_general x9 -> x0, matrix products: 71.9 us -> none  [the longest x8 64.4 us: sensor_block(): jnp.einsum('skhb,skb->hs', picked, coeffs, preferred_element_type=jnp.flo...]
    pallas_call x0 -> x1, Pallas kernels: none -> 67.3 us  [body(): pl.pallas_call(run, out_shape=(jax.ShapeDtypeStruct((hours, sens * n_sky)...]
    all_gather x2 -> x0, waiting for transfers between devices: 60 us -> none  [the longest x1 60 us: body(): tables = lax.all_gather(bsdf, 'sensor', axis=0, tiled=True)]
    convert_element_type x1 -> x0, local copies, waits for them, and re-layouts: 15.9 us -> none  [body(): transmitted = jnp.einsum('whb,wcb->whc', irradiance, chosen, preferred_el...]
    all_to_all x1 -> x0, local copies, waits for them, and re-layouts: 11 us -> none  [body(): lax.all_to_all(transmitted, 'sky', split_axis=1, concat_axis=0, tiled=True)]
    squeeze x8 -> x0, local copies, waits for them, and re-layouts: 8.6 us -> none  [body(): parts_out = lax.map(sensor_block, (rows_blocked, ids_blocked))]
  transfers between devices with their start and end apart: 3 -> 0, of which waited for: 1 -> 0; matrix products, arithmetic and copies ran while one was open for 2% -> 0% of each run, Pallas kernels for 0% -> 0%
where the time goes in v1:
time: 83.5 us; the launch traced here: 83.4 us
  Pallas kernels  67.3 us (81%)
  between operations  14 us (17%)
  local copies, waits for them, and re-layouts  1.81 us (2%)
    pallas_call x1, Pallas kernels, body(): pl.pallas_call(run, out_shape=(jax.ShapeDtypeStruct((hours, sens * n_sky)...  67.3 us

profile of v1, /device:TPU:1, one launch (start us, length us, event | category | flops | bytes accessed | tf_op | source)
XLA Modules:
  0.0 83.4 jit_solution(3400625792401998663)
XLA Ops:
  6.5 67.3 %shard_map.75 = (f32[32,256]{1,0:T(8,128)S(1)}, f32[8,128]{1,0:T(8,128)}) custom-call(bf16[32,146]{1,0:T(8,128)(2,1)} %bitcast.70, bf16[145,40,146]{2,1,0:T(8,128)(2,1)} %bitcast.64, bf16[145,145]{1,0:T(8,128)(2,1)} %bitcast.68, s32[1,40]{1,0:T(1,128)} %refs_3_.1, bf16[512,145]{1,0:T(8,128)(2,1)} %bitcast.66, s32[16,32]{1,0:T(8,128)} %bitcast.71, ...), custom_call_target="tpu_custom_call" | custom-call | tf_op jit(solution)/shard_map/pallas_call | solution.py:337
  73.8 1.2 %slice.3 = f32[1,1]{1,0:T(1,128)} slice(f32[8,128]{1,0:T(8,128)} %get-tuple-element.61), slice={[0:1], [0:1]} | slice | bytes 8 | tf_op jit(solution)/shard_map/slice | solution.py:372
  75.7 0.2 conditional.1
  75.9 0.6 copy.54

commit v2 on v0

v2 whole, which is shorter than its diff:
```python
import jax
import jax.numpy as jnp
from jax import lax
from jax.experimental import pallas as pl
from jax.experimental.pallas import tpu as pltpu
from jax.sharding import PartitionSpec as P

F32 = jnp.float32
BF16 = jnp.bfloat16
MESH = pl.DeviceIdType.MESH
ROWS = 48
FOLD = 16
STEP = 24
NOTE = 80
HUGE = 1e30


def up(n, m):
    return -(-n // m) * m


def iota(shape, dim):
    return lax.broadcasted_iota(jnp.int32, shape, dim)


def dot(a, b, dims=((1,), (0,))):
    return lax.dot_general(a, b, (dims, ((), ())), preferred_element_type=F32)


def fold(x, rows):
    parts = [x[g * rows : (g + 1) * rows] for g in range(x.shape[0] // rows)]
    return sum([p if g == 0 else pltpu.roll(p, g * STEP, 1) for g, p in enumerate(parts)])


def unfold(x, groups):
    return jnp.concatenate([x if g == 0 else pltpu.roll(x, 128 - g * STEP, 1) for g in range(groups)], axis=0)


def kernel(dims, first, sky_ref, day_hbm, bsdf_ref, ids_ref, view_ref, vis_ref, counts_ref, round_ref, out_ref, flag_ref,
           day, wide, days, mats, own, tail, store, skies, vpad, rank, send, got, dense, part, light, outs, ins, fown, fgot,
           day_sem, loc_sem, z_send, z_recv, s_send, s_recv, v_send, v_recv, p_send, p_recv, b_send, b_recv,
           f_send, f_recv, o_send, o_recv):
    n_sky, n_sen, bins, patches, wins, sens, slots, hours = dims
    nz = n_sen // 2
    kb = up(bins, 16)
    half = (kb + 32) // 2
    entries = sens * slots
    me = lax.axis_index("sky")
    mine = lax.axis_index("sensor")
    z, core = mine // 2, lax.rem(mine, 2)
    sibling = z * 2 + (1 - core)
    near, far = me, lax.rem(me + nz // 2, nz)

    def plane(shift, c):
        return lax.rem(z + shift + nz, nz) * 2 + c

    barrier = pltpu.get_barrier_semaphore()

    def greet(other_sky, other_sensor):
        pl.semaphore_signal(barrier, inc=1, device_id=(other_sky, other_sensor), device_id_type=MESH)

    def greet_sky(k, c):
        greet(lax.rem(me + k, n_sky), mine)
        return c

    lax.fori_loop(1, n_sky, greet_sky, 0)
    greet(me, sibling)
    if first:
        greet(me, plane(near, 1 - core))
    near_other, far_other = near != 0, far != 0

    @pl.when(near_other)
    def _():
        greet(me, plane(near, core))

    @pl.when(far_other)
    def _():
        greet(me, plane(far, core))

    day_copy = pltpu.make_async_copy(day_hbm, day, day_sem)
    day_copy.start()

    own[0:kb, :] = jnp.zeros((kb, 128), BF16)
    own[0:bins, :] = bsdf_ref[:, 0:128]
    tail[...] = jnp.zeros(tail.shape, F32)
    tail[0:bins, 0 : bins - 128] = bsdf_ref[:, 128:bins].astype(F32)
    own[kb : kb + 32, :] = fold(tail[...], 32).astype(BF16)
    skies[me] = jnp.zeros(skies.shape[1:], BF16)
    skies[me, :, 0:patches] = sky_ref[...]

    vis = vis_ref[...]
    owner = vis // wins
    local = vis - owner * wins
    spread = (lax.rem(iota((slots, entries), 1), slots) == iota((slots, entries), 0)).astype(BF16)
    sensor_of = iota((sens, entries), 1) // slots == iota((sens, entries), 0)

    def flat(x):
        return jnp.sum(jnp.where(sensor_of, dot(x.astype(F32).astype(BF16), spread), 0.0), axis=0, keepdims=True)

    owner_row, local_row = flat(owner), flat(local)
    slot_row = lax.rem(iota((1, entries), 1), slots).astype(F32)
    sens_row = (iota((1, entries), 1) // slots).astype(F32)
    counts = jnp.broadcast_to(counts_ref[...].astype(F32), (16, sens)).astype(BF16)
    count_row = dot(counts, sensor_of.astype(BF16))[0:1]
    live = slot_row < count_row
    goes = jnp.logical_and(iota((n_sky, entries), 0).astype(F32) == owner_row, live)
    goes_f = goes.astype(F32)
    earlier = (iota((entries, entries), 0) < iota((entries, entries), 1)).astype(BF16)
    ranks = dot(goes_f.astype(BF16), earlier) - (0 if first else (round_ref[0, 0] * ROWS).astype(F32))
    rank[...] = jnp.where(jnp.logical_and(goes, ranks >= 0.0), ranks, -1000.0)
    most = jnp.max(jnp.sum(goes_f, axis=1, keepdims=True), axis=0, keepdims=True)
    over = jnp.where(most > ROWS, 1.0, 0.0)

    pl.semaphore_wait(barrier, n_sky + (1 if first else 0) + near_other.astype(jnp.int32) + far_other.astype(jnp.int32))

    def along(i, to, c):
        return pltpu.make_async_remote_copy(
            src_ref=own.at[pl.ds(i * half, half)], dst_ref=store.at[core, me, i], send_sem=z_send.at[i],
            recv_sem=z_recv.at[i], device_id=(me, plane(-to, c)), device_id_type=MESH)

    def stay(i):
        return pltpu.make_async_copy(own.at[pl.ds(i * half, half)], store.at[core, me, i], z_recv.at[i])

    for i, to, other in ((0, near, near_other), (1, far, far_other)):

        @pl.when(other)
        def _(i=i, to=to):
            along(i, to, core).start()

        @pl.when(jnp.logical_not(other))
        def _(i=i):
            stay(i).start()

    def sky_copy(q, slot):
        return pltpu.make_async_remote_copy(
            src_ref=skies.at[slot], dst_ref=skies.at[slot], send_sem=s_send.at[q], recv_sem=s_recv.at[slot],
            device_id=(q, mine), device_id_type=MESH)

    vpad[...] = jnp.zeros(vpad.shape, BF16)
    vpad[:, 0:bins] = view_ref[...]
    note_row = iota((FOLD, entries), 0)
    notes = jnp.where(note_row == 0, local_row + 1.0, jnp.where(note_row == 1, sens_row, 0.0)).astype(BF16)
    place = (iota((128, entries), 0) - NOTE).astype(F32)
    at_flag = jnp.logical_and(iota((FOLD, 128), 0) == 2, iota((FOLD, 128), 1) >= NOTE)
    flag_note = jnp.where(at_flag, over, 0.0)

    def message(q, slot):
        return pltpu.make_async_remote_copy(
            src_ref=send.at[q], dst_ref=got.at[slot], send_sem=v_send.at[q], recv_sem=v_recv.at[slot],
            device_id=(q, mine), device_id_type=MESH)

    def pack(q):
        pick = (place == rank[pl.ds(q, 1), :]).astype(BF16)
        rows = dot(pick[NOTE : NOTE + ROWS], vpad[...])
        send[q, 0:ROWS, :] = rows[:, 0:128].astype(BF16)
        notes_at = dot(notes, pick, ((1,), (1,)))
        send[q, ROWS : ROWS + FOLD, :] = (fold(rows[:, 128:256], FOLD) + notes_at + flag_note).astype(BF16)

    def put(k, c):
        q = lax.rem(me + k, n_sky)
        pack(q)
        message(q, me).start()
        sky_copy(q, me).start()
        return c

    lax.fori_loop(1, n_sky, put, 0)
    pack(me)
    keep = pltpu.make_async_copy(send.at[me], got.at[me], loc_sem)
    keep.start()

    def in_plane(q, slot):
        return pltpu.make_async_remote_copy(
            src_ref=store.at[core, slot], dst_ref=store.at[core, slot], send_sem=p_send.at[q], recv_sem=p_recv.at[slot],
            device_id=(q, mine), device_id_type=MESH)

    def across(c, slot):
        return pltpu.make_async_remote_copy(
            src_ref=store.at[c, slot], dst_ref=store.at[c, slot], send_sem=b_send.at[slot], recv_sem=b_recv.at[slot],
            device_id=(me, sibling), device_id_type=MESH)

    for i in range(2):
        stay(i).wait()

    def put_plane(k, c):
        in_plane(lax.rem(me + k, n_sky), me).start()
        return c

    lax.fori_loop(1, n_sky, put_plane, 0)
    across(core, me).start()

    wide[1] = jnp.zeros(wide.shape[1:], F32)
    wide[0, bins * wins :, :] = jnp.zeros((wide.shape[1] - bins * wins, 128), F32)
    day_copy.wait()

    def widen(b, c):
        x = day[b].astype(F32)
        rows = pl.ds(pl.multiple_of(b * wins, 8), wins)
        wide[0, rows, :] = x[:, 0:128]
        wide[1, rows, 0 : patches - 128] = x[:, 128:patches]
        return c

    lax.fori_loop(0, bins, widen, 0, unroll=5 if bins % 5 == 0 else 1)

    def by_window(w, c):
        for i in range(2):
            days[w, :, i * 128 : i * 128 + 128] = wide[i, pl.ds(w, kb, stride=wins), :].astype(BF16)
        return c

    lax.fori_loop(0, wins, by_window, 0)

    keep.wait()

    def await_message(k, c):
        q = lax.rem(me + k, n_sky)
        message(q, q).wait_recv()
        return c

    lax.fori_loop(1, n_sky, await_message, 0)
    if first:
        flags = jnp.zeros((FOLD, 128), F32)
        for q in range(n_sky):
            flags = jnp.maximum(flags, got[q, ROWS : ROWS + FOLD, :].astype(F32))
        fown[...] = jnp.broadcast_to(flags[2:3, 127:128], fown.shape).astype(BF16)

        def flag_copy(i, c):
            return pltpu.make_async_remote_copy(
                src_ref=fown, dst_ref=fgot.at[i], send_sem=f_send.at[i], recv_sem=f_recv.at[i],
                device_id=(me, plane(-near, c)), device_id_type=MESH)

        flag_stay = pltpu.make_async_copy(fown, fgot.at[0], f_recv.at[0])

        @pl.when(near_other)
        def _():
            flag_copy(0, core).start()

        @pl.when(jnp.logical_not(near_other))
        def _():
            flag_stay.start()

        flag_copy(1, 1 - core).start()

    which = iota((wins * sens, ROWS), 0).astype(F32)

    def unpack(q, c):
        folded = got[q, ROWS : ROWS + FOLD, :].astype(F32)
        note = pltpu.roll(folded, 128 - NOTE, 1)[:, 0:ROWS]
        code = note[0:1] * float(sens) + note[1:2] - float(sens)
        pick = (which == code).astype(BF16)
        rows = jnp.concatenate([got[q, 0:ROWS, :], unfold(folded, ROWS // FOLD).astype(BF16)], axis=1)
        placed = dot(pick, rows).astype(BF16).reshape(wins, sens, 256)
        dense[:, pl.ds(pl.multiple_of(q * sens, sens), sens), :] = placed
        return c

    lax.fori_loop(0, n_sky, unpack, 0)

    def relay(k, c):
        q = lax.rem(me + k, n_sky)
        in_plane(q, q).wait_recv()
        across(core, q).start()
        return c

    lax.fori_loop(1, n_sky, relay, 0)

    def await_across(q, c):
        across(1 - core, q).wait_recv()
        return c

    lax.fori_loop(0, n_sky, await_across, 0)

    def through(w, c):
        table = ids_ref[0, w]
        away = table // 2 - z + nz
        a = store[table % 2, away % nz, 0]
        b = store[table % 2, (away + nz // 2) % nz, 1]
        ends = unfold(b[half - 32 :].astype(F32), kb // 32).astype(BF16)
        whole = jnp.concatenate([jnp.concatenate([a, b[0 : half - 32]], axis=0), ends], axis=1)
        mats[w] = dot(whole[:, 0:kb], days[w]).astype(BF16)
        return c

    lax.fori_loop(0, wins, through, 0, unroll=4)

    part[...] = jnp.zeros(part.shape, F32)
    group = 8 if wins % 8 == 0 else 1

    def gather(g, c):
        acc = part[...]
        for i in range(group):
            w = g * group + i
            acc = acc + dot(dense[w][:, 0:kb], mats[w])
        part[...] = acc
        return c

    lax.fori_loop(0, wins // group, gather, 0)

    def await_sky(k, c):
        q = lax.rem(me + k, n_sky)
        sky_copy(q, q).wait_recv()
        return c

    lax.fori_loop(1, n_sky, await_sky, 0)
    a = part[...]
    high = a.astype(BF16)
    low = (a - high.astype(F32)).astype(BF16)
    every = skies[...].reshape(n_sky * hours, 256)
    shares = dot(every, high, ((1,), (1,))) + dot(every, low, ((1,), (1,)))
    if first:
        flag_stay.wait()
        flag_copy(1, 1 - core).wait_recv()
        seen = jnp.maximum(fgot[0], fgot[1]).astype(F32)[0:1, 0:1]
        shares = jnp.where(seen > 0.0, HUGE, shares)
    light[...] = shares.reshape(light.shape)
    outs[...] = shares.astype(BF16).reshape(outs.shape)

    def share(q, slot):
        return pltpu.make_async_remote_copy(
            src_ref=outs.at[q], dst_ref=ins.at[slot], send_sem=o_send.at[q], recv_sem=o_recv.at[slot],
            device_id=(q, mine), device_id_type=MESH)

    def put_share(k, c):
        share(lax.rem(me + k, n_sky), me).start()
        return c

    lax.fori_loop(1, n_sky, put_share, 0)

    def add(k, total):
        q = lax.rem(me + k, n_sky)
        share(q, q).wait_recv()
        return total + ins[q].astype(F32)

    total = lax.fori_loop(1, n_sky, add, light[me])
    out_ref[...] = total
    flag_ref[0, 0] = jnp.max(total[0:8, 0:128])

    for i, other in enumerate((near_other, far_other)):

        @pl.when(other)
        def _(i=i):
            along(i, near, core).wait_send()

    if first:

        @pl.when(near_other)
        def _():
            flag_copy(0, core).wait_send()

        flag_copy(1, 1 - core).wait_send()

    def drain(k, c):
        q = lax.rem(me + k, n_sky)
        message(q, me).wait_send()
        sky_copy(q, me).wait_send()
        in_plane(q, me).wait_send()
        share(q, me).wait_send()
        return c

    lax.fori_loop(1, n_sky, drain, 0)

    def drain_across(q, c):
        across(core, q).wait_send()
        return c

    lax.fori_loop(0, n_sky, drain_across, 0)


def body(sky, daylight, bsdf, bsdf_ids, view, visible, counts):
    n_sky, n_sen = lax.axis_size("sky"), lax.axis_size("sensor")
    patches, hours = sky.shape
    _, wins, bins, _ = daylight.shape
    _, sens, slots, _ = view.shape
    kb, entries = up(bins, 32), sens * slots
    dims = (n_sky, n_sen, bins, patches, wins, sens, slots, hours)
    vmem, smem = pl.BlockSpec(memory_space=pltpu.VMEM), pl.BlockSpec(memory_space=pltpu.SMEM)
    dma, all_sens = pltpu.SemaphoreType.DMA, sens * n_sky
    args = (sky.T, jnp.transpose(daylight[0], (1, 0, 2)), bsdf[0], bsdf_ids, view[0].reshape(entries, bins), visible[0], counts)

    def call(first, number):
        def run(*refs):
            kernel(dims, first, *refs)

        return pl.pallas_call(
            run,
            out_shape=(jax.ShapeDtypeStruct((hours, all_sens), F32), jax.ShapeDtypeStruct((1, 1), F32)),
            in_specs=[vmem, pl.BlockSpec(memory_space=pl.ANY), vmem, smem, vmem, vmem, vmem, smem],
            out_specs=(vmem, smem),
            scratch_shapes=[
                pltpu.VMEM((bins, wins, patches), BF16),
                pltpu.VMEM((2, kb * wins, 128), F32),
                pltpu.VMEM((wins, kb, 256), BF16),
                pltpu.VMEM((wins, kb, 256), BF16),
                pltpu.VMEM((kb + 32, 128), BF16),
                pltpu.VMEM((kb, 128), F32),
                pltpu.VMEM((2, n_sky, 2, (kb + 32) // 2, 128), BF16),
                pltpu.VMEM((n_sky, hours, 256), BF16),
                pltpu.VMEM((entries, 256), BF16),
                pltpu.VMEM((n_sky, entries), F32),
                pltpu.VMEM((n_sky, ROWS + FOLD, 128), BF16),
                pltpu.VMEM((n_sky, ROWS + FOLD, 128), BF16),
                pltpu.VMEM((wins, all_sens, 256), BF16),
                pltpu.VMEM((all_sens, 256), F32),
                pltpu.VMEM((n_sky, hours, all_sens), F32),
                pltpu.VMEM((n_sky, hours, all_sens), BF16),
                pltpu.VMEM((n_sky, hours, all_sens), BF16),
                pltpu.VMEM((16, 128), BF16),
                pltpu.VMEM((2, 16, 128), BF16),
                dma, dma, dma((2,)), dma((2,)), dma((n_sky,)), dma((n_sky,)), dma((n_sky,)), dma((n_sky,)),
                dma((n_sky,)), dma((n_sky,)), dma((n_sky,)), dma((n_sky,)), dma((2,)), dma((2,)), dma((n_sky,)), dma((n_sky,)),
            ],
            compiler_params=pltpu.CompilerParams(
                collective_id=0 if first else 1, has_side_effects=True, vmem_limit_bytes=56 * 2**20),
        )(*args, jnp.reshape(number, (1, 1)).astype(jnp.int32))

    out, flag = call(True, jnp.zeros((), jnp.int32))

    def in_rounds():
        rounds = -(-entries // ROWS)
        return lax.fori_loop(0, rounds, lambda i, acc: acc + call(False, i)[0], jnp.zeros_like(out))

    return lax.cond(flag[0, 0] > HUGE / 1e6, in_rounds, lambda: out)[None]


def solution(mesh):
    in_specs = (
        P(None, "sky"),
        P("sensor", "sky", None, None),
        P("sensor", None, None),
        P("sensor", "sky"),
        P("sensor", "sky", None, None),
        P("sensor", "sky", None),
        P("sensor", "sky"),
    )
    return jax.shard_map(body, mesh=mesh, in_specs=in_specs, out_specs=P("sensor", "sky", None), check_vma=False)
```

time: 540 us -> 54.6 us (0.10); the launches traced: 534 us -> 54.4 us
  blocking collectives: 204 us -> 0 us
  local copies, waits for them, and re-layouts: 174 us -> 1.4 us
  matrix products: 71.9 us -> 0 us
  waiting for transfers between devices: 60.7 us -> 0 us
  Pallas kernels: 0 us -> 52.3 us
  between operations: 14.9 us -> 0.73 us
  starting transfers between devices: 6.59 us -> 0 us
    all_gather x2 -> x0, blocking collectives: 204 us -> none  [the longest x1 185 us: body(): lax.all_gather(visible, 'sky', axis=1, tiled=True)]
    gather x9 -> x0, local copies, waits for them, and re-layouts: 135 us -> none  [the longest x8 131 us: sensor_block(): picked = light[window_ids]]
    dot_general x9 -> x0, matrix products: 71.9 us -> none  [the longest x8 64.4 us: sensor_block(): jnp.einsum('skhb,skb->hs', picked, coeffs, preferred_element_type=jnp.flo...]
    all_gather x2 -> x0, waiting for transfers between devices: 60 us -> none  [the longest x1 60 us: body(): tables = lax.all_gather(bsdf, 'sensor', axis=0, tiled=True)]
    pallas_call x0 -> x1, Pallas kernels: none -> 52.3 us  [call(): pl.pallas_call(run, out_shape=(jax.ShapeDtypeStruct((hours, all_sens), F3...]
    convert_element_type x1 -> x0, local copies, waits for them, and re-layouts: 15.9 us -> none  [body(): transmitted = jnp.einsum('whb,wcb->whc', irradiance, chosen, preferred_el...]
    all_to_all x1 -> x0, local copies, waits for them, and re-layouts: 11 us -> none  [body(): lax.all_to_all(transmitted, 'sky', split_axis=1, concat_axis=0, tiled=True)]
    squeeze x8 -> x0, local copies, waits for them, and re-layouts: 8.6 us -> none  [body(): parts_out = lax.map(sensor_block, (rows_blocked, ids_blocked))]
  transfers between devices with their start and end apart: 3 -> 0, of which waited for: 1 -> 0; matrix products, arithmetic and copies ran while one was open for 2% -> 0% of each run, Pallas kernels for 0% -> 0%
where the time goes in v2:
time: 54.6 us; the launch traced here: 54.4 us
  Pallas kernels  52.3 us (96%)
  local copies, waits for them, and re-layouts  1.4 us (3%)
  between operations  0.73 us (1%)
    pallas_call x1, Pallas kernels, call(): pl.pallas_call(run, out_shape=(jax.ShapeDtypeStruct((hours, all_sens), F3...  52.3 us
    unnamed x15, local copies, waits for them, and re-layouts  1.4 us

profile of v2, /device:TPU:1, one launch (start us, length us, event | category | flops | bytes accessed | tf_op | source)
XLA Modules:
  0.0 54.4 jit_solution(6812864673586862035)
XLA Ops:
  0.0 0.0 copy-start.6
  0.0 0.0 copy-start.5
  0.0 0.0 copy-start.4
  0.0 0.0 copy-start.1
  0.0 0.0 copy-start.2
  0.0 0.0 copy-start
  0.0 0.0 copy-start.3
  0.0 52.3 %shard_map.75 = (f32[32,256]{1,0:T(8,128)}, f32[1,1]{1,0:T(1,128)}) custom-call(bf16[32,146]{1,0:T(8,128)(2,1)} %bitcast.19, bf16[145,40,146]{2,1,0:T(8,128)(2,1)} %bitcast.13, bf16[145,145]{1,0:T(8,128)(2,1)} %bitcast.17, s32[1,40]{1,0:T(1,128)} %refs_3_.1, bf16[512,145]{1,0:T(8,128)(2,1)} %bitcast.15, s32[16,32]{1,0:T(8,128)} %bitcast.21, ...), custom_call_target="tpu_custom_call" | custom-call | tf_op jit(solution)/shard_map/pallas_call | solution.py:380
  53.0 0.0 copy-done.6
  53.0 0.0 copy-done.5
  53.0 0.0 copy-done.4
  53.0 0.0 copy-done.1
  53.0 0.0 copy-done.2
  53.0 0.0 copy-done
  53.0 0.0 copy-done.3
  53.1 1.4 %copy.19 = f32[1,32,256]{2,1,0:T(8,128)} copy(f32[1,32,256]{2,1,0:T(8,128)} %get-tuple-element.177) | data formatting | bytes 65536
  (1 shorter events, 0.0 us)
Async XLA Ops:
  0.0 53.0 %copy-start.6 = (s32[1,16]{1,0:T(1,128)S(1)}, s32[1,16]{1,0:T(1,128)}, u32[]{:S(2)}) copy-start(s32[1,16]{1,0:T(1,128)} %refs_6_.1) | copy-start | bytes 196
  0.0 53.0 %copy-start.5 = (s32[1,40]{1,0:T(1,128)S(1)}, s32[1,40]{1,0:T(1,128)}, u32[]{:S(2)}) copy-start(s32[1,40]{1,0:T(1,128)} %refs_3_.1) | copy-start | bytes 484
  0.0 53.0 %copy-start.4 = (s32[1,16,32]{2,1,0:T(8,128)S(1)}, s32[1,16,32]{2,1,0:T(8,128)}, u32[]{:S(2)}) copy-start(s32[1,16,32]{2,1,0:T(8,128)} %param.16) | copy-start | bytes 6148
  0.0 53.0 %copy-start.1 = (bf16[1,16,32,145]{3,2,1,0:T(8,128)(2,1)S(1)}, bf16[1,16,32,145]{3,2,1,0:T(8,128)(2,1)}, u32[]{:S(2)}) copy-start(bf16[1,16,32,145]{3,2,1,0:T(8,128)(2,1)} %param.15) | copy-start | bytes 445444
  0.0 53.0 %copy-start.2 = (bf16[1,145,145]{2,1,0:T(8,128)(2,1)S(1)}, bf16[1,145,145]{2,1,0:T(8,128)(2,1)}, u32[]{:S(2)}) copy-start(bf16[1,145,145]{2,1,0:T(8,128)(2,1)} %param.13) | copy-start | bytes 126154
  0.0 53.0 %copy-start = (bf16[1,40,145,146]{3,1,2,0:T(8,128)(2,1)S(1)}, bf16[1,40,145,146]{3,1,2,0:T(8,128)(2,1)}, u32[]{:S(2)}) copy-start(bf16[1,40,145,146]{3,1,2,0:T(8,128)(2,1)} %param.12) | copy-start | bytes 5080804
  0.0 53.0 %copy-start.3 = (bf16[146,32]{0,1:T(8,128)(2,1)S(1)}, bf16[146,32]{0,1:T(8,128)(2,1)}, u32[]{:S(2)}) copy-start(bf16[146,32]{0,1:T(8,128)(2,1)} %param.11) | copy-start | bytes 28036

commit v3 on v2

--- a/solution.py
+++ b/solution.py
@@ -36,9 +36,9 @@
     return jnp.concatenate([x if g == 0 else pltpu.roll(x, 128 - g * STEP, 1) for g in range(groups)], axis=0)
 
 
-def kernel(dims, first, sky_ref, day_hbm, bsdf_ref, ids_ref, view_ref, vis_ref, counts_ref, round_ref, out_ref, flag_ref,
-           day, wide, days, mats, own, tail, store, skies, vpad, rank, send, got, dense, part, light, outs, ins, fown, fgot,
-           day_sem, loc_sem, z_send, z_recv, s_send, s_recv, v_send, v_recv, p_send, p_recv, b_send, b_recv,
+def kernel(dims, first, round_ref, sky_hbm, day_hbm, bsdf_hbm, ids_hbm, view_hbm, vis_hbm, counts_hbm, out_ref, flag_ref,
+           sky_ref, day, bsdf_ref, ids_ref, view_ref, vis_ref, counts_ref, wide, days, mats, own, tail, store, skies, vpad, rank, send, got, dense, part, light, outs, ins, fown, fgot,
+           in_sem, loc_sem, z_send, z_recv, v_send, v_recv, p_send, p_recv, b_send, b_recv,
            f_send, f_recv, o_send, o_recv):
     n_sky, n_sen, bins, patches, wins, sens, slots, hours = dims
     nz = n_sen // 2
@@ -54,6 +54,14 @@
     def plane(shift, c):
         return lax.rem(z + shift + nz, nz) * 2 + c
 
+    load_sky, load_day, load_bsdf, load_ids, load_view, load_vis, load_counts = [
+        pltpu.make_async_copy(src, dst, in_sem.at[i])
+        for i, (src, dst) in enumerate((
+            (sky_hbm, sky_ref), (day_hbm, day), (bsdf_hbm, bsdf_ref), (ids_hbm, ids_ref), (view_hbm, view_ref),
+            (vis_hbm, vis_ref), (counts_hbm, counts_ref)))
+    ]
+    for load in (load_bsdf, load_vis, load_counts, load_view, load_sky, load_ids, load_day):
+        load.start()
     barrier = pltpu.get_barrier_semaphore()
 
     def greet(other_sky, other_sensor):
@@ -77,17 +85,16 @@
     def _():
         greet(me, plane(far, core))
 
-    day_copy = pltpu.make_async_copy(day_hbm, day, day_sem)
-    day_copy.start()
-
     own[0:kb, :] = jnp.zeros((kb, 128), BF16)
+    load_bsdf.wait()
     own[0:bins, :] = bsdf_ref[:, 0:128]
     tail[...] = jnp.zeros(tail.shape, F32)
     tail[0:bins, 0 : bins - 128] = bsdf_ref[:, 128:bins].astype(F32)
     own[kb : kb + 32, :] = fold(tail[...], 32).astype(BF16)
-    skies[me] = jnp.zeros(skies.shape[1:], BF16)
-    skies[me, :, 0:patches] = sky_ref[...]
-
+    ins[me] = jnp.zeros(ins.shape[1:], BF16)
+
+    load_vis.wait()
+    load_counts.wait()
     vis = vis_ref[...]
     owner = vis // wins
     local = vis - owner * wins
@@ -131,11 +138,12 @@
         def _(i=i):
             stay(i).start()
 
-    def sky_copy(q, slot):
-        return pltpu.make_async_remote_copy(
-            src_ref=skies.at[slot], dst_ref=skies.at[slot], send_sem=s_send.at[q], recv_sem=s_recv.at[slot],
-            device_id=(q, mine), device_id_type=MESH)
-
+    sky_at = ROWS + FOLD
+    load_view.wait()
+    load_sky.wait()
+    tail[0:hours, :] = jnp.zeros((hours, 128), F32)
+    tail[0:hours, 0 : patches - 128] = sky_ref[:, 128:patches].astype(F32)
+    sky_ends = fold(tail[0:hours, :], FOLD).astype(BF16)
     vpad[...] = jnp.zeros(vpad.shape, BF16)
     vpad[:, 0:bins] = view_ref[...]
     note_row = iota((FOLD, entries), 0)
@@ -144,38 +152,42 @@
     at_flag = jnp.logical_and(iota((FOLD, 128), 0) == 2, iota((FOLD, 128), 1) >= NOTE)
     flag_note = jnp.where(at_flag, over, 0.0)
 
-    def message(q, slot):
+    def message(q):
         return pltpu.make_async_remote_copy(
-            src_ref=send.at[q], dst_ref=got.at[slot], send_sem=v_send.at[q], recv_sem=v_recv.at[slot],
+            src_ref=send.at[q], dst_ref=got.at[me], send_sem=v_send, recv_sem=v_recv,
             device_id=(q, mine), device_id_type=MESH)
 
-    def pack(q):
+    def all_of(ref, sem, n):
+        return pltpu.make_async_copy(ref.at[pl.ds(0, n)], ref.at[pl.ds(0, n)], sem)
+
+    def pack(q, c):
         pick = (place == rank[pl.ds(q, 1), :]).astype(BF16)
         rows = dot(pick[NOTE : NOTE + ROWS], vpad[...])
         send[q, 0:ROWS, :] = rows[:, 0:128].astype(BF16)
         notes_at = dot(notes, pick, ((1,), (1,)))
         send[q, ROWS : ROWS + FOLD, :] = (fold(rows[:, 128:256], FOLD) + notes_at + flag_note).astype(BF16)
+        send[q, sky_at : sky_at + hours, :] = sky_ref[:, 0:128]
+        send[q, sky_at + hours :, :] = sky_ends
+        return c
+
+    lax.fori_loop(0, n_sky, pack, 0, unroll=4 if n_sky % 4 == 0 else 1)
 
     def put(k, c):
-        q = lax.rem(me + k, n_sky)
-        pack(q)
-        message(q, me).start()
-        sky_copy(q, me).start()
+        message(lax.rem(me + k, n_sky)).start()
         return c
 
     lax.fori_loop(1, n_sky, put, 0)
-    pack(me)
     keep = pltpu.make_async_copy(send.at[me], got.at[me], loc_sem)
     keep.start()
 
     def in_plane(q, slot):
         return pltpu.make_async_remote_copy(
-            src_ref=store.at[core, slot], dst_ref=store.at[core, slot], send_sem=p_send.at[q], recv_sem=p_recv.at[slot],
+            src_ref=store.at[core, slot], dst_ref=store.at[core, slot], send_sem=p_send, recv_sem=p_recv.at[slot],
             device_id=(q, mine), device_id_type=MESH)
 
     def across(c, slot):
         return pltpu.make_async_remote_copy(
-            src_ref=store.at[c, slot], dst_ref=store.at[c, slot], send_sem=b_send.at[slot], recv_sem=b_recv.at[slot],
+            src_ref=store.at[c, slot], dst_ref=store.at[c, slot], send_sem=b_send, recv_sem=b_recv,
             device_id=(me, sibling), device_id_type=MESH)
 
     for i in range(2):
@@ -190,7 +202,7 @@
 
     wide[1] = jnp.zeros(wide.shape[1:], F32)
     wide[0, bins * wins :, :] = jnp.zeros((wide.shape[1] - bins * wins, 128), F32)
-    day_copy.wait()
+    load_day.wait()
 
     def widen(b, c):
         x = day[b].astype(F32)
@@ -210,12 +222,7 @@
 
     keep.wait()
 
-    def await_message(k, c):
-        q = lax.rem(me + k, n_sky)
-        message(q, q).wait_recv()
-        return c
-
-    lax.fori_loop(1, n_sky, await_message, 0)
+    all_of(got, v_recv, n_sky - 1).wait()
     if first:
         flags = jnp.zeros((FOLD, 128), F32)
         for q in range(n_sky):
@@ -249,6 +256,8 @@
         rows = jnp.concatenate([got[q, 0:ROWS, :], unfold(folded, ROWS // FOLD).astype(BF16)], axis=1)
         placed = dot(pick, rows).astype(BF16).reshape(wins, sens, 256)
         dense[:, pl.ds(pl.multiple_of(q * sens, sens), sens), :] = placed
+        skies[q, :, 0:128] = got[q, sky_at : sky_at + hours, :]
+        skies[q, :, 128:256] = unfold(got[q, sky_at + hours :, :].astype(F32), hours // FOLD).astype(BF16)
         return c
 
     lax.fori_loop(0, n_sky, unpack, 0)
@@ -261,11 +270,8 @@
 
     lax.fori_loop(1, n_sky, relay, 0)
 
-    def await_across(q, c):
-        across(1 - core, q).wait_recv()
-        return c
-
-    lax.fori_loop(0, n_sky, await_across, 0)
+    load_ids.wait()
+    all_of(store.at[1 - core], b_recv, n_sky).wait()
 
     def through(w, c):
         table = ids_ref[0, w]
@@ -277,7 +283,7 @@
         mats[w] = dot(whole[:, 0:kb], days[w]).astype(BF16)
         return c
 
-    lax.fori_loop(0, wins, through, 0, unroll=4)
+    lax.fori_loop(0, wins, through, 0, unroll=8 if wins % 8 == 0 else 1)
 
     part[...] = jnp.zeros(part.shape, F32)
     group = 8 if wins % 8 == 0 else 1
@@ -292,12 +298,6 @@
 
     lax.fori_loop(0, wins // group, gather, 0)
 
-    def await_sky(k, c):
-        q = lax.rem(me + k, n_sky)
-        sky_copy(q, q).wait_recv()
-        return c
-
-    lax.fori_loop(1, n_sky, await_sky, 0)
     a = part[...]
     high = a.astype(BF16)
     low = (a - high.astype(F32)).astype(BF16)
@@ -311,23 +311,19 @@
     light[...] = shares.reshape(light.shape)
     outs[...] = shares.astype(BF16).reshape(outs.shape)
 
-    def share(q, slot):
-        return pltpu.make_async_remote_copy(
-            src_ref=outs.at[q], dst_ref=ins.at[slot], send_sem=o_send.at[q], recv_sem=o_recv.at[slot],
-            device_id=(q, mine), device_id_type=MESH)
-
     def put_share(k, c):
-        share(lax.rem(me + k, n_sky), me).start()
+        q = lax.rem(me + k, n_sky)
+        pltpu.make_async_remote_copy(
+            src_ref=outs.at[q], dst_ref=ins.at[me], send_sem=o_send, recv_sem=o_recv,
+            device_id=(q, mine), device_id_type=MESH).start()
         return c
 
     lax.fori_loop(1, n_sky, put_share, 0)
 
-    def add(k, total):
-        q = lax.rem(me + k, n_sky)
-        share(q, q).wait_recv()
-        return total + ins[q].astype(F32)
-
-    total = lax.fori_loop(1, n_sky, add, light[me])
+    all_of(ins, o_recv, n_sky - 1).wait()
+    total = light[me]
+    for q in range(n_sky):
+        total = total + ins[q].astype(F32)
     out_ref[...] = total
     flag_ref[0, 0] = jnp.max(total[0:8, 0:128])
 
@@ -345,21 +341,10 @@
 
         flag_copy(1, 1 - core).wait_send()
 
-    def drain(k, c):
-        q = lax.rem(me + k, n_sky)
-        message(q, me).wait_send()
-        sky_copy(q, me).wait_send()
-        in_plane(q, me).wait_send()
-        share(q, me).wait_send()
-        return c
-
-    lax.fori_loop(1, n_sky, drain, 0)
-
-    def drain_across(q, c):
-        across(core, q).wait_send()
-        return c
-
-    lax.fori_loop(0, n_sky, drain_across, 0)
+    all_of(send, v_send, n_sky - 1).wait()
+    all_of(store.at[core], p_send, n_sky - 1).wait()
+    all_of(store.at[core], b_send, n_sky).wait()
+    all_of(outs, o_send, n_sky - 1).wait()
 
 
 def body(sky, daylight, bsdf, bsdf_ids, view, visible, counts):
@@ -375,15 +360,23 @@
 
     def call(first, number):
         def run(*refs):
+            if first:
+                refs = (None,) + refs
             kernel(dims, first, *refs)
 
         return pl.pallas_call(
             run,
             out_shape=(jax.ShapeDtypeStruct((hours, all_sens), F32), jax.ShapeDtypeStruct((1, 1), F32)),
-            in_specs=[vmem, pl.BlockSpec(memory_space=pl.ANY), vmem, smem, vmem, vmem, vmem, smem],
+            in_specs=([] if first else [smem]) + [pl.BlockSpec(memory_space=pl.ANY)] * 7,
             out_specs=(vmem, smem),
             scratch_shapes=[
+                pltpu.VMEM((hours, patches), BF16),
                 pltpu.VMEM((bins, wins, patches), BF16),
+                pltpu.VMEM((bins, bins), BF16),
+                pltpu.SMEM((1, wins), jnp.int32),
+                pltpu.VMEM((entries, bins), BF16),
+                pltpu.VMEM((sens, slots), jnp.int32),
+                pltpu.VMEM((1, sens), jnp.int32),
                 pltpu.VMEM((2, kb * wins, 128), F32),
                 pltpu.VMEM((wins, kb, 256), BF16),
                 pltpu.VMEM((wins, kb, 256), BF16),
@@ -393,8 +386,8 @@
                 pltpu.VMEM((n_sky, hours, 256), BF16),
                 pltpu.VMEM((entries, 256), BF16),
                 pltpu.VMEM((n_sky, entries), F32),
-                pltpu.VMEM((n_sky, ROWS + FOLD, 128), BF16),
-                pltpu.VMEM((n_sky, ROWS + FOLD, 128), BF16),
+                pltpu.VMEM((n_sky, ROWS + 2 * FOLD + hours, 128), BF16),
+                pltpu.VMEM((n_sky, ROWS + 2 * FOLD + hours, 128), BF16),
                 pltpu.VMEM((wins, all_sens, 256), BF16),
                 pltpu.VMEM((all_sens, 256), F32),
                 pltpu.VMEM((n_sky, hours, all_sens), F32),
@@ -402,14 +395,13 @@
                 pltpu.VMEM((n_sky, hours, all_sens), BF16),
                 pltpu.VMEM((16, 128), BF16),
                 pltpu.VMEM((2, 16, 128), BF16),
-                dma, dma, dma((2,)), dma((2,)), dma((n_sky,)), dma((n_sky,)), dma((n_sky,)), dma((n_sky,)),
-                dma((n_sky,)), dma((n_sky,)), dma((n_sky,)), dma((n_sky,)), dma((2,)), dma((2,)), dma((n_sky,)), dma((n_sky,)),
+                dma((7,)), dma, dma((2,)), dma((2,)), dma, dma, dma, dma((n_sky,)), dma, dma, dma((2,)), dma((2,)), dma, dma,
             ],
             compiler_params=pltpu.CompilerParams(
                 collective_id=0 if first else 1, has_side_effects=True, vmem_limit_bytes=56 * 2**20),
-        )(*args, jnp.reshape(number, (1, 1)).astype(jnp.int32))
-
-    out, flag = call(True, jnp.zeros((), jnp.int32))
+        )(*(() if first else (jnp.reshape(number, (1, 1)).astype(jnp.int32),)), *args)
+
+    out, flag = call(True, 0)
 
     def in_rounds():
         rounds = -(-entries // ROWS)

time: 54.6 us -> 51.3 us (0.940)
  Pallas kernels: 52.3 us -> 49 us
    pallas_call x1, Pallas kernels: 52.3 us -> 49 us  [call(): pl.pallas_call(run, out_shape=(jax.ShapeDtypeStruct((hours, all_sens), F3...]
where the time goes in v3:
time: 51.3 us; the launch traced here: 51.1 us
  Pallas kernels  49 us (96%)
  local copies, waits for them, and re-layouts  1.4 us (3%)
  between operations  0.73 us (1%)
    pallas_call x1, Pallas kernels, call(): pl.pallas_call(run, out_shape=(jax.ShapeDtypeStruct((hours, all_sens), F3...  49 us
    unnamed x15, local copies, waits for them, and re-layouts  1.4 us

profile of v3, /device:TPU:1, one launch (start us, length us, event | category | flops | bytes accessed | tf_op | source)
XLA Modules:
  0.0 51.1 jit_solution(9639214674697396925)
XLA Ops:
  0.0 0.0 copy-start.6
  0.0 0.0 copy-start.5
  0.0 0.0 copy-start.4
  0.0 0.0 copy-start.1
  0.0 0.0 copy-start.2
  0.0 0.0 copy-start
  0.0 0.0 copy-start.3
  0.0 49.0 %shard_map.75 = (f32[32,256]{1,0:T(8,128)}, f32[1,1]{1,0:T(1,128)}) custom-call(bf16[32,146]{1,0:T(8,128)(2,1)} %bitcast.19, bf16[145,40,146]{2,1,0:T(8,128)(2,1)} %bitcast.13, bf16[145,145]{1,0:T(8,128)(2,1)} %bitcast.17, s32[1,40]{1,0:T(1,128)} %refs_3_.1, bf16[512,145]{1,0:T(8,128)(2,1)} %bitcast.15, s32[16,32]{1,0:T(8,128)} %bitcast.21, s32[1,16]{1,0:T(1,128)} %refs_6_.1), custom_call_target="tpu_custom_call" | custom-call | tf_op jit(solution)/shard_map/pallas_call | solution.py:367
  49.7 0.0 copy-done.6
  49.7 0.0 copy-done.5
  49.7 0.0 copy-done.4
  49.7 0.0 copy-done.1
  49.7 0.0 copy-done.2
  49.7 0.0 copy-done
  49.7 0.0 copy-done.3
  49.7 1.4 %copy.19 = f32[1,32,256]{2,1,0:T(8,128)} copy(f32[1,32,256]{2,1,0:T(8,128)} %get-tuple-element.177) | data formatting | bytes 65536
  (1 shorter events, 0.0 us)
Async XLA Ops:
  0.0 49.7 %copy-start.6 = (s32[1,16]{1,0:T(1,128)S(1)}, s32[1,16]{1,0:T(1,128)}, u32[]{:S(2)}) copy-start(s32[1,16]{1,0:T(1,128)} %refs_6_.1) | copy-start | bytes 196
  0.0 49.7 %copy-start.5 = (s32[1,40]{1,0:T(1,128)S(1)}, s32[1,40]{1,0:T(1,128)}, u32[]{:S(2)}) copy-start(s32[1,40]{1,0:T(1,128)} %refs_3_.1) | copy-start | bytes 484
  0.0 49.7 %copy-start.4 = (s32[1,16,32]{2,1,0:T(8,128)S(1)}, s32[1,16,32]{2,1,0:T(8,128)}, u32[]{:S(2)}) copy-start(s32[1,16,32]{2,1,0:T(8,128)} %param.16) | copy-start | bytes 6148
  0.0 49.7 %copy-start.1 = (bf16[1,16,32,145]{3,2,1,0:T(8,128)(2,1)S(1)}, bf16[1,16,32,145]{3,2,1,0:T(8,128)(2,1)}, u32[]{:S(2)}) copy-start(bf16[1,16,32,145]{3,2,1,0:T(8,128)(2,1)} %param.15) | copy-start | bytes 445444
  0.0 49.7 %copy-start.2 = (bf16[1,145,145]{2,1,0:T(8,128)(2,1)S(1)}, bf16[1,145,145]{2,1,0:T(8,128)(2,1)}, u32[]{:S(2)}) copy-start(bf16[1,145,145]{2,1,0:T(8,128)(2,1)} %param.13) | copy-start | bytes 126154
  0.0 49.7 %copy-start = (bf16[1,40,145,146]{3,1,2,0:T(8,128)(2,1)S(1)}, bf16[1,40,145,146]{3,1,2,0:T(8,128)(2,1)}, u32[]{:S(2)}) copy-start(bf16[1,40,145,146]{3,1,2,0:T(8,128)(2,1)} %param.12) | copy-start | bytes 5080804
  0.0 49.7 %copy-start.3 = (bf16[146,32]{0,1:T(8,128)(2,1)S(1)}, bf16[146,32]{0,1:T(8,128)(2,1)}, u32[]{:S(2)}) copy-start(bf16[146,32]{0,1:T(8,128)(2,1)} %param.11) | copy-start | bytes 28036

commit v4 on v3

--- a/solution.py
+++ b/solution.py
@@ -37,8 +37,8 @@
 
 
 def kernel(dims, first, round_ref, sky_hbm, day_hbm, bsdf_hbm, ids_hbm, view_hbm, vis_hbm, counts_hbm, out_ref, flag_ref,
-           sky_ref, day, bsdf_ref, ids_ref, view_ref, vis_ref, counts_ref, wide, days, mats, own, tail, store, skies, vpad, rank, send, got, dense, part, light, outs, ins, fown, fgot,
-           in_sem, loc_sem, z_send, z_recv, v_send, v_recv, p_send, p_recv, b_send, b_recv,
+           sky_ref, day, bsdf_ref, ids_ref, view_ref, vis_ref, counts_ref, wide, days, mats, own, tail, store, hours_in, skies, vpad, rank, send, got, dense, light, outs, ins, fown, fgot,
+           in_sem, loc_sem, z_send, z_recv, s_send, s_recv, v_send, v_recv, p_send, p_recv, b_send, b_recv,
            f_send, f_recv, o_send, o_recv):
     n_sky, n_sen, bins, patches, wins, sens, slots, hours = dims
     nz = n_sen // 2
@@ -60,8 +60,9 @@
             (sky_hbm, sky_ref), (day_hbm, day), (bsdf_hbm, bsdf_ref), (ids_hbm, ids_ref), (view_hbm, view_ref),
             (vis_hbm, vis_ref), (counts_hbm, counts_ref)))
     ]
-    for load in (load_bsdf, load_vis, load_counts, load_view, load_sky, load_ids, load_day):
-        load.start()
+    def all_of(ref, sem, n):
+        return pltpu.make_async_copy(ref.at[pl.ds(0, n)], ref.at[pl.ds(0, n)], sem)
+
     barrier = pltpu.get_barrier_semaphore()
 
     def greet(other_sky, other_sensor):
@@ -71,10 +72,6 @@
         greet(lax.rem(me + k, n_sky), mine)
         return c
 
-    lax.fori_loop(1, n_sky, greet_sky, 0)
-    greet(me, sibling)
-    if first:
-        greet(me, plane(near, 1 - core))
     near_other, far_other = near != 0, far != 0
 
     @pl.when(near_other)
@@ -84,6 +81,14 @@
     @pl.when(far_other)
     def _():
         greet(me, plane(far, core))
+
+    if first:
+        greet(me, plane(near, 1 - core))
+    lax.fori_loop(1, n_sky, greet_sky, 0)
+    greet(me, sibling)
+
+    for load in (load_bsdf, load_vis, load_counts, load_view, load_sky, load_ids, load_day):
+        load.start()
 
     own[0:kb, :] = jnp.zeros((kb, 128), BF16)
     load_bsdf.wait()
@@ -138,12 +143,7 @@
         def _(i=i):
             stay(i).start()
 
-    sky_at = ROWS + FOLD
     load_view.wait()
-    load_sky.wait()
-    tail[0:hours, :] = jnp.zeros((hours, 128), F32)
-    tail[0:hours, 0 : patches - 128] = sky_ref[:, 128:patches].astype(F32)
-    sky_ends = fold(tail[0:hours, :], FOLD).astype(BF16)
     vpad[...] = jnp.zeros(vpad.shape, BF16)
     vpad[:, 0:bins] = view_ref[...]
     note_row = iota((FOLD, entries), 0)
@@ -157,17 +157,12 @@
             src_ref=send.at[q], dst_ref=got.at[me], send_sem=v_send, recv_sem=v_recv,
             device_id=(q, mine), device_id_type=MESH)
 
-    def all_of(ref, sem, n):
-        return pltpu.make_async_copy(ref.at[pl.ds(0, n)], ref.at[pl.ds(0, n)], sem)
-
     def pack(q, c):
         pick = (place == rank[pl.ds(q, 1), :]).astype(BF16)
         rows = dot(pick[NOTE : NOTE + ROWS], vpad[...])
         send[q, 0:ROWS, :] = rows[:, 0:128].astype(BF16)
         notes_at = dot(notes, pick, ((1,), (1,)))
         send[q, ROWS : ROWS + FOLD, :] = (fold(rows[:, 128:256], FOLD) + notes_at + flag_note).astype(BF16)
-        send[q, sky_at : sky_at + hours, :] = sky_ref[:, 0:128]
-        send[q, sky_at + hours :, :] = sky_ends
         return c
 
     lax.fori_loop(0, n_sky, pack, 0, unroll=4 if n_sky % 4 == 0 else 1)
@@ -199,6 +194,20 @@
 
     lax.fori_loop(1, n_sky, put_plane, 0)
     across(core, me).start()
+
+    load_sky.wait()
+    tail[0:hours, :] = jnp.zeros((hours, 128), F32)
+    tail[0:hours, 0 : patches - 128] = sky_ref[:, 128:patches].astype(F32)
+    hours_in[me, 0:hours, :] = sky_ref[:, 0:128]
+    hours_in[me, hours:, :] = fold(tail[0:hours, :], FOLD).astype(BF16)
+
+    def put_hours(k, c):
+        pltpu.make_async_remote_copy(
+            src_ref=hours_in.at[me], dst_ref=hours_in.at[me], send_sem=s_send, recv_sem=s_recv,
+            device_id=(lax.rem(me + k, n_sky), mine), device_id_type=MESH).start()
+        return c
+
+    lax.fori_loop(1, n_sky, put_hours, 0)
 
     wide[1] = jnp.zeros(wide.shape[1:], F32)
     wide[0, bins * wins :, :] = jnp.zeros((wide.shape[1] - bins * wins, 128), F32)
@@ -246,21 +255,34 @@
 
         flag_copy(1, 1 - core).start()
 
-    which = iota((wins * sens, ROWS), 0).astype(F32)
+    which = iota((wins // 4 * sens, ROWS), 0).astype(F32)
+    keep_tail = iota((ROWS, 128), 1) < kb - 128
 
     def unpack(q, c):
         folded = got[q, ROWS : ROWS + FOLD, :].astype(F32)
         note = pltpu.roll(folded, 128 - NOTE, 1)[:, 0:ROWS]
-        code = note[0:1] * float(sens) + note[1:2] - float(sens)
-        pick = (which == code).astype(BF16)
-        rows = jnp.concatenate([got[q, 0:ROWS, :], unfold(folded, ROWS // FOLD).astype(BF16)], axis=1)
-        placed = dot(pick, rows).astype(BF16).reshape(wins, sens, 256)
-        dense[:, pl.ds(pl.multiple_of(q * sens, sens), sens), :] = placed
-        skies[q, :, 0:128] = got[q, sky_at : sky_at + hours, :]
-        skies[q, :, 128:256] = unfold(got[q, sky_at + hours :, :].astype(F32), hours // FOLD).astype(BF16)
-        return c
-
-    lax.fori_loop(0, n_sky, unpack, 0)
+        window = note[0:1] - 1.0
+        four = jnp.floor(window * 0.25)
+        place_in = window - 4.0 * four
+        target = four * float(sens) + note[1:2]
+        ends = jnp.where(keep_tail, unfold(folded, ROWS // FOLD), 0.0)
+        rows = jnp.concatenate([got[q, 0:ROWS, :].astype(F32), ends], axis=1)
+        parts = []
+        for m in range(4):
+            pick = (which == jnp.where(place_in == float(m), target, -1.0)).astype(BF16)
+            moved = rows if m == 0 else pltpu.roll(rows, m * (kb - 128), 1)
+            parts.append(dot(pick, moved.astype(BF16)))
+        at = pl.ds(pl.multiple_of(q * sens, sens), sens)
+        for t in range(5):
+            tile = parts[t][:, 0:128] if t < 4 else parts[3][:, 128:256]
+            if 0 < t < 4:
+                tile = tile + parts[t - 1][:, 128:256]
+            tile = tile.astype(BF16).reshape(wins // 8, 2, sens, 128)
+            for h in range(2):
+                dense[:, at, h * 4 * kb + t * 128 : h * 4 * kb + t * 128 + 128] = tile[:, h]
+        return c
+
+    lax.fori_loop(0, n_sky, unpack, 0, unroll=2 if n_sky % 2 == 0 else 1)
 
     def relay(k, c):
         q = lax.rem(me + k, n_sky)
@@ -270,6 +292,14 @@
 
     lax.fori_loop(1, n_sky, relay, 0)
 
+    all_of(hours_in, s_recv, n_sky - 1).wait()
+
+    def unfold_hours(q, c):
+        skies[q, :, 0:128] = hours_in[q, 0:hours, :]
+        skies[q, :, 128:256] = unfold(hours_in[q, hours:, :].astype(F32), hours // FOLD).astype(BF16)
+        return c
+
+    lax.fori_loop(0, n_sky, unfold_hours, 0, unroll=4 if n_sky % 4 == 0 else 1)
     load_ids.wait()
     all_of(store.at[1 - core], b_recv, n_sky).wait()
 
@@ -285,20 +315,10 @@
 
     lax.fori_loop(0, wins, through, 0, unroll=8 if wins % 8 == 0 else 1)
 
-    part[...] = jnp.zeros(part.shape, F32)
-    group = 8 if wins % 8 == 0 else 1
-
-    def gather(g, c):
-        acc = part[...]
-        for i in range(group):
-            w = g * group + i
-            acc = acc + dot(dense[w][:, 0:kb], mats[w])
-        part[...] = acc
-        return c
-
-    lax.fori_loop(0, wins // group, gather, 0)
-
-    a = part[...]
+    a = jnp.zeros((sens * n_sky, 256), F32)
+    for g in range(wins // 8):
+        a = a + dot(dense[g], mats[g * 8 : g * 8 + 8].reshape(8 * kb, 256))
+
     high = a.astype(BF16)
     low = (a - high.astype(F32)).astype(BF16)
     every = skies[...].reshape(n_sky * hours, 256)
@@ -342,6 +362,7 @@
         flag_copy(1, 1 - core).wait_send()
 
     all_of(send, v_send, n_sky - 1).wait()
+    all_of(hours_in, s_send, n_sky - 1).wait()
     all_of(store.at[core], p_send, n_sky - 1).wait()
     all_of(store.at[core], b_send, n_sky).wait()
     all_of(outs, o_send, n_sky - 1).wait()
@@ -383,19 +404,19 @@
                 pltpu.VMEM((kb + 32, 128), BF16),
                 pltpu.VMEM((kb, 128), F32),
                 pltpu.VMEM((2, n_sky, 2, (kb + 32) // 2, 128), BF16),
+                pltpu.VMEM((n_sky, hours + FOLD, 128), BF16),
                 pltpu.VMEM((n_sky, hours, 256), BF16),
                 pltpu.VMEM((entries, 256), BF16),
                 pltpu.VMEM((n_sky, entries), F32),
-                pltpu.VMEM((n_sky, ROWS + 2 * FOLD + hours, 128), BF16),
-                pltpu.VMEM((n_sky, ROWS + 2 * FOLD + hours, 128), BF16),
-                pltpu.VMEM((wins, all_sens, 256), BF16),
-                pltpu.VMEM((all_sens, 256), F32),
+                pltpu.VMEM((n_sky, ROWS + FOLD, 128), BF16),
+                pltpu.VMEM((n_sky, ROWS + FOLD, 128), BF16),
+                pltpu.VMEM((wins // 8, all_sens, 8 * kb), BF16),
                 pltpu.VMEM((n_sky, hours, all_sens), F32),
                 pltpu.VMEM((n_sky, hours, all_sens), BF16),
                 pltpu.VMEM((n_sky, hours, all_sens), BF16),
                 pltpu.VMEM((16, 128), BF16),
                 pltpu.VMEM((2, 16, 128), BF16),
-                dma((7,)), dma, dma((2,)), dma((2,)), dma, dma, dma, dma((n_sky,)), dma, dma, dma((2,)), dma((2,)), dma, dma,
+                dma((7,)), dma, dma((2,)), dma((2,)), dma, dma, dma, dma, dma, dma((n_sky,)), dma, dma, dma((2,)), dma((2,)), dma, dma,
             ],
             compiler_params=pltpu.CompilerParams(
                 collective_id=0 if first else 1, has_side_effects=True, vmem_limit_bytes=56 * 2**20),

time: 51.3 us -> 49.2 us (0.959)
  Pallas kernels: 49 us -> 46.9 us
    pallas_call x1, Pallas kernels: 49 us -> 46.9 us  [call(): pl.pallas_call(run, out_shape=(jax.ShapeDtypeStruct((hours, all_sens), F3...]
where the time goes in v4:
time: 49.2 us; the launch traced here: 49 us
  Pallas kernels  46.9 us (95%)
  local copies, waits for them, and re-layouts  1.4 us (3%)
  between operations  0.73 us (1%)
    pallas_call x1, Pallas kernels, call(): pl.pallas_call(run, out_shape=(jax.ShapeDtypeStruct((hours, all_sens), F3...  46.9 us
    unnamed x15, local copies, waits for them, and re-layouts  1.4 us

profile of v4, /device:TPU:1, one launch (start us, length us, event | category | flops | bytes accessed | tf_op | source)
XLA Modules:
  0.0 49.0 jit_solution(8496901099400412612)
XLA Ops:
  0.0 0.0 copy-start.6
  0.0 0.0 copy-start.5
  0.0 0.0 copy-start.4
  0.0 0.0 copy-start.1
  0.0 0.0 copy-start.2
  0.0 0.0 copy-start
  0.0 0.0 copy-start.3
  0.0 46.9 %shard_map.75 = (f32[32,256]{1,0:T(8,128)}, f32[1,1]{1,0:T(1,128)}) custom-call(bf16[32,146]{1,0:T(8,128)(2,1)} %bitcast.19, bf16[145,40,146]{2,1,0:T(8,128)(2,1)} %bitcast.13, bf16[145,145]{1,0:T(8,128)(2,1)} %bitcast.17, s32[1,40]{1,0:T(1,128)} %refs_3_.1, bf16[512,145]{1,0:T(8,128)(2,1)} %bitcast.15, s32[16,32]{1,0:T(8,128)} %bitcast.21, s32[1,16]{1,0:T(1,128)} %refs_6_.1), custom_call_target="tpu_custom_call" | custom-call | tf_op jit(solution)/shard_map/pallas_call | solution.py:388
  47.6 0.0 copy-done.6
  47.6 0.0 copy-done.5
  47.6 0.0 copy-done.4
  47.6 0.0 copy-done.1
  47.6 0.0 copy-done.2
  47.6 0.0 copy-done
  47.6 0.0 copy-done.3
  47.6 1.4 %copy.19 = f32[1,32,256]{2,1,0:T(8,128)} copy(f32[1,32,256]{2,1,0:T(8,128)} %get-tuple-element.177) | data formatting | bytes 65536
  (1 shorter events, 0.0 us)
Async XLA Ops:
  0.0 47.6 %copy-start.6 = (s32[1,16]{1,0:T(1,128)S(1)}, s32[1,16]{1,0:T(1,128)}, u32[]{:S(2)}) copy-start(s32[1,16]{1,0:T(1,128)} %refs_6_.1) | copy-start | bytes 196
  0.0 47.6 %copy-start.5 = (s32[1,40]{1,0:T(1,128)S(1)}, s32[1,40]{1,0:T(1,128)}, u32[]{:S(2)}) copy-start(s32[1,40]{1,0:T(1,128)} %refs_3_.1) | copy-start | bytes 484
  0.0 47.6 %copy-start.4 = (s32[1,16,32]{2,1,0:T(8,128)S(1)}, s32[1,16,32]{2,1,0:T(8,128)}, u32[]{:S(2)}) copy-start(s32[1,16,32]{2,1,0:T(8,128)} %param.16) | copy-start | bytes 6148
  0.0 47.6 %copy-start.1 = (bf16[1,16,32,145]{3,2,1,0:T(8,128)(2,1)S(1)}, bf16[1,16,32,145]{3,2,1,0:T(8,128)(2,1)}, u32[]{:S(2)}) copy-start(bf16[1,16,32,145]{3,2,1,0:T(8,128)(2,1)} %param.15) | copy-start | bytes 445444
  0.0 47.6 %copy-start.2 = (bf16[1,145,145]{2,1,0:T(8,128)(2,1)S(1)}, bf16[1,145,145]{2,1,0:T(8,128)(2,1)}, u32[]{:S(2)}) copy-start(bf16[1,145,145]{2,1,0:T(8,128)(2,1)} %param.13) | copy-start | bytes 126154
  0.0 47.6 %copy-start = (bf16[1,40,145,146]{3,1,2,0:T(8,128)(2,1)S(1)}, bf16[1,40,145,146]{3,1,2,0:T(8,128)(2,1)}, u32[]{:S(2)}) copy-start(bf16[1,40,145,146]{3,1,2,0:T(8,128)(2,1)} %param.12) | copy-start | bytes 5080804
  0.0 47.6 %copy-start.3 = (bf16[146,32]{0,1:T(8,128)(2,1)S(1)}, bf16[146,32]{0,1:T(8,128)(2,1)}, u32[]{:S(2)}) copy-start(bf16[146,32]{0,1:T(8,128)(2,1)} %param.11) | copy-start | bytes 28036

commit v5 on v4

--- a/solution.py
+++ b/solution.py
@@ -60,6 +60,7 @@
             (sky_hbm, sky_ref), (day_hbm, day), (bsdf_hbm, bsdf_ref), (ids_hbm, ids_ref), (view_hbm, view_ref),
             (vis_hbm, vis_ref), (counts_hbm, counts_ref)))
     ]
+
     def all_of(ref, sem, n):
         return pltpu.make_async_copy(ref.at[pl.ds(0, n)], ref.at[pl.ds(0, n)], sem)
 
@@ -72,6 +73,11 @@
         greet(lax.rem(me + k, n_sky), mine)
         return c
 
+    if n_sky == 16:
+        steps = sorted(range(1, 16), key=lambda k: -min(k // 4, 4 - k // 4) - min(k % 4, 4 - k % 4))
+        others = [lax.rem(me // 4 + k // 4, 4) * 4 + lax.rem(lax.rem(me, 4) + k % 4, 4) for k in steps]
+    else:
+        others = [lax.rem(me + k, n_sky) for k in range(1, n_sky)]
     near_other, far_other = near != 0, far != 0
 
     @pl.when(near_other)
@@ -123,26 +129,6 @@
     most = jnp.max(jnp.sum(goes_f, axis=1, keepdims=True), axis=0, keepdims=True)
     over = jnp.where(most > ROWS, 1.0, 0.0)
 
-    pl.semaphore_wait(barrier, n_sky + (1 if first else 0) + near_other.astype(jnp.int32) + far_other.astype(jnp.int32))
-
-    def along(i, to, c):
-        return pltpu.make_async_remote_copy(
-            src_ref=own.at[pl.ds(i * half, half)], dst_ref=store.at[core, me, i], send_sem=z_send.at[i],
-            recv_sem=z_recv.at[i], device_id=(me, plane(-to, c)), device_id_type=MESH)
-
-    def stay(i):
-        return pltpu.make_async_copy(own.at[pl.ds(i * half, half)], store.at[core, me, i], z_recv.at[i])
-
-    for i, to, other in ((0, near, near_other), (1, far, far_other)):
-
-        @pl.when(other)
-        def _(i=i, to=to):
-            along(i, to, core).start()
-
-        @pl.when(jnp.logical_not(other))
-        def _(i=i):
-            stay(i).start()
-
     load_view.wait()
     vpad[...] = jnp.zeros(vpad.shape, BF16)
     vpad[:, 0:bins] = view_ref[...]
@@ -152,11 +138,6 @@
     at_flag = jnp.logical_and(iota((FOLD, 128), 0) == 2, iota((FOLD, 128), 1) >= NOTE)
     flag_note = jnp.where(at_flag, over, 0.0)
 
-    def message(q):
-        return pltpu.make_async_remote_copy(
-            src_ref=send.at[q], dst_ref=got.at[me], send_sem=v_send, recv_sem=v_recv,
-            device_id=(q, mine), device_id_type=MESH)
-
     def pack(q, c):
         pick = (place == rank[pl.ds(q, 1), :]).astype(BF16)
         rows = dot(pick[NOTE : NOTE + ROWS], vpad[...])
@@ -167,6 +148,31 @@
 
     lax.fori_loop(0, n_sky, pack, 0, unroll=4 if n_sky % 4 == 0 else 1)
 
+    pl.semaphore_wait(barrier, n_sky + (1 if first else 0) + near_other.astype(jnp.int32) + far_other.astype(jnp.int32))
+
+    def along(i, to, c):
+        return pltpu.make_async_remote_copy(
+            src_ref=own.at[pl.ds(i * half, half)], dst_ref=store.at[core, me, i], send_sem=z_send.at[i],
+            recv_sem=z_recv.at[i], device_id=(me, plane(-to, c)), device_id_type=MESH)
+
+    def stay(i):
+        return pltpu.make_async_copy(own.at[pl.ds(i * half, half)], store.at[core, me, i], z_recv.at[i])
+
+    for i, to, other in ((0, near, near_other), (1, far, far_other)):
+
+        @pl.when(other)
+        def _(i=i, to=to):
+            along(i, to, core).start()
+
+        @pl.when(jnp.logical_not(other))
+        def _(i=i):
+            stay(i).start()
+
+    def message(q):
+        return pltpu.make_async_remote_copy(
+            src_ref=send.at[q], dst_ref=got.at[me], send_sem=v_send, recv_sem=v_recv,
+            device_id=(q, mine), device_id_type=MESH)
+
     def put(k, c):
         message(lax.rem(me + k, n_sky)).start()
         return c
@@ -188,11 +194,8 @@
     for i in range(2):
         stay(i).wait()
 
-    def put_plane(k, c):
-        in_plane(lax.rem(me + k, n_sky), me).start()
-        return c
-
-    lax.fori_loop(1, n_sky, put_plane, 0)
+    for q in others:
+        in_plane(q, me).start()
     across(core, me).start()
 
     load_sky.wait()
@@ -284,13 +287,9 @@
 
     lax.fori_loop(0, n_sky, unpack, 0, unroll=2 if n_sky % 2 == 0 else 1)
 
-    def relay(k, c):
-        q = lax.rem(me + k, n_sky)
+    for q in others[::-1]:
         in_plane(q, q).wait_recv()
         across(core, q).start()
-        return c
-
-    lax.fori_loop(1, n_sky, relay, 0)
 
     all_of(hours_in, s_recv, n_sky - 1).wait()
 
@@ -313,7 +312,7 @@
         mats[w] = dot(whole[:, 0:kb], days[w]).astype(BF16)
         return c
 
-    lax.fori_loop(0, wins, through, 0, unroll=8 if wins % 8 == 0 else 1)
+    lax.fori_loop(0, wins, through, 0, unroll=20 if wins % 20 == 0 else 1)
 
     a = jnp.zeros((sens * n_sky, 256), F32)
     for g in range(wins // 8):
@@ -331,14 +330,10 @@
     light[...] = shares.reshape(light.shape)
     outs[...] = shares.astype(BF16).reshape(outs.shape)
 
-    def put_share(k, c):
-        q = lax.rem(me + k, n_sky)
+    for q in others:
         pltpu.make_async_remote_copy(
             src_ref=outs.at[q], dst_ref=ins.at[me], send_sem=o_send, recv_sem=o_recv,
             device_id=(q, mine), device_id_type=MESH).start()
-        return c
-
-    lax.fori_loop(1, n_sky, put_share, 0)
 
     all_of(ins, o_recv, n_sky - 1).wait()
     total = light[me]

time: 49.2 us -> 47.9 us (0.974)
  Pallas kernels: 46.9 us -> 45.6 us
    pallas_call x1, Pallas kernels: 46.9 us -> 45.6 us  [call(): pl.pallas_call(run, out_shape=(jax.ShapeDtypeStruct((hours, all_sens), F3...]
where the time goes in v5:
time: 47.9 us; the launch traced here: 47.7 us
  Pallas kernels  45.6 us (95%)
  local copies, waits for them, and re-layouts  1.4 us (3%)
  between operations  0.73 us (2%)
    pallas_call x1, Pallas kernels, call(): pl.pallas_call(run, out_shape=(jax.ShapeDtypeStruct((hours, all_sens), F3...  45.6 us
    unnamed x15, local copies, waits for them, and re-layouts  1.4 us

profile of v5, /device:TPU:1, one launch (start us, length us, event | category | flops | bytes accessed | tf_op | source)
XLA Modules:
  0.0 47.7 jit_solution(10849092714773265090)
XLA Ops:
  0.0 0.0 copy-start.6
  0.0 0.0 copy-start.5
  0.0 0.0 copy-start.4
  0.0 0.0 copy-start.1
  0.0 0.0 copy-start.2
  0.0 0.0 copy-start
  0.0 0.0 copy-start.3
  0.0 45.6 %shard_map.75 = (f32[32,256]{1,0:T(8,128)}, f32[1,1]{1,0:T(1,128)}) custom-call(bf16[32,146]{1,0:T(8,128)(2,1)} %bitcast.19, bf16[145,40,146]{2,1,0:T(8,128)(2,1)} %bitcast.13, bf16[145,145]{1,0:T(8,128)(2,1)} %bitcast.17, s32[1,40]{1,0:T(1,128)} %refs_3_.1, bf16[512,145]{1,0:T(8,128)(2,1)} %bitcast.15, s32[16,32]{1,0:T(8,128)} %bitcast.21, s32[1,16]{1,0:T(1,128)} %refs_6_.1), custom_call_target="tpu_custom_call" | custom-call | tf_op jit(solution)/shard_map/pallas_call | solution.py:383
  46.3 0.0 copy-done.6
  46.3 0.0 copy-done.5
  46.3 0.0 copy-done.4
  46.3 0.0 copy-done.1
  46.3 0.0 copy-done.2
  46.3 0.0 copy-done
  46.3 0.0 copy-done.3
  46.3 1.4 %copy.19 = f32[1,32,256]{2,1,0:T(8,128)} copy(f32[1,32,256]{2,1,0:T(8,128)} %get-tuple-element.177) | data formatting | bytes 65536
  (1 shorter events, 0.0 us)
Async XLA Ops:
  0.0 46.3 %copy-start.6 = (s32[1,16]{1,0:T(1,128)S(1)}, s32[1,16]{1,0:T(1,128)}, u32[]{:S(2)}) copy-start(s32[1,16]{1,0:T(1,128)} %refs_6_.1) | copy-start | bytes 196
  0.0 46.3 %copy-start.5 = (s32[1,40]{1,0:T(1,128)S(1)}, s32[1,40]{1,0:T(1,128)}, u32[]{:S(2)}) copy-start(s32[1,40]{1,0:T(1,128)} %refs_3_.1) | copy-start | bytes 484
  0.0 46.3 %copy-start.4 = (s32[1,16,32]{2,1,0:T(8,128)S(1)}, s32[1,16,32]{2,1,0:T(8,128)}, u32[]{:S(2)}) copy-start(s32[1,16,32]{2,1,0:T(8,128)} %param.16) | copy-start | bytes 6148
  0.0 46.3 %copy-start.1 = (bf16[1,16,32,145]{3,2,1,0:T(8,128)(2,1)S(1)}, bf16[1,16,32,145]{3,2,1,0:T(8,128)(2,1)}, u32[]{:S(2)}) copy-start(bf16[1,16,32,145]{3,2,1,0:T(8,128)(2,1)} %param.15) | copy-start | bytes 445444
  0.0 46.3 %copy-start.2 = (bf16[1,145,145]{2,1,0:T(8,128)(2,1)S(1)}, bf16[1,145,145]{2,1,0:T(8,128)(2,1)}, u32[]{:S(2)}) copy-start(bf16[1,145,145]{2,1,0:T(8,128)(2,1)} %param.13) | copy-start | bytes 126154
  0.0 46.3 %copy-start = (bf16[1,40,145,146]{3,1,2,0:T(8,128)(2,1)S(1)}, bf16[1,40,145,146]{3,1,2,0:T(8,128)(2,1)}, u32[]{:S(2)}) copy-start(bf16[1,40,145,146]{3,1,2,0:T(8,128)(2,1)} %param.12) | copy-start | bytes 5080804
  0.0 46.3 %copy-start.3 = (bf16[146,32]{0,1:T(8,128)(2,1)S(1)}, bf16[146,32]{0,1:T(8,128)(2,1)}, u32[]{:S(2)}) copy-start(bf16[146,32]{0,1:T(8,128)(2,1)} %param.11) | copy-start | bytes 28036
